TPU v7x, 32 devices: a whole 2x2x4 slice. The times are simulated.
32 devices in a mesh: grp: 2 (over x), ctx: 16 (over z, y, core).
Axes of the slice: x: 2, y: 2, z: 4, core: 2. Of those that a mesh axis runs over, the one named last changes fastest.
Arguments:
- queries: bfloat16 [16384, 2048], P(('grp', 'ctx')), parts along dimension 0, may hold values from -7 to 7
- keys: bfloat16 [16384, 512], P(('grp', 'ctx')), parts along dimension 0, may hold values from -6 to 6
- values: bfloat16 [16384, 512], P(('grp', 'ctx')), parts along dimension 0, may hold values from -6 to 6
- out_grad: bfloat16 [16384, 2048], P(('grp', 'ctx')), parts along dimension 0, may hold values from -6 to 6
- doc_starts: int32 [16], P('grp'), parts along dimension 0, may hold values from 0 to 7423, as said below
- block_lists: int32 [128, 6], P(('grp', 'ctx')), parts along dimension 0, may hold values from -1 to 63, as said below
Outputs:
- attended: bfloat16 [16384, 2048], P(('grp', 'ctx')), parts along dimension 0
- grad_queries: bfloat16 [16384, 2048], P(('grp', 'ctx')), parts along dimension 0
- grad_keys: bfloat16 [16384, 512], P(('grp', 'ctx')), parts along dimension 0
- grad_values: bfloat16 [16384, 512], P(('grp', 'ctx')), parts along dimension 0
There are 2 independent parts, one for each index of `grp`. A program takes and returns all parts, laid end to end along the dimension named above; each array names one. Nothing has to cross between parts.
Inputs may be any that keep to these rules, and one draw needn't show every extreme that they name: `block_lists`: row b lists block b first, then further distinct blocks before b that lie in the document of b's last token and among the blocks of b's device or of the 2 devices before it, then -1 in every slot left empty; the last row is full. `doc_starts`: Increasing, the first entry 0.
All inputs are finite; a program needn't handle non-finite values.
Results may differ from a plain program's by a relative error of at most 0.029.
Values may be sent and summed in bfloat16 or wider, within the bound.
A program may use at most 128 MiB of HBM per device.

v0:
```python
import jax
import jax.numpy as jnp
from jax import lax
from jax.sharding import PartitionSpec as P

HD = 128
HEADS = 16
KV_HEADS = 4
BLOCK = 128
R_DEV = 2


def shifted(value, axis, steps):
    count = lax.axis_size(axis)
    initial, last = (max(0, -steps), min(count, count - steps))
    return lax.ppermute(value, axis, [(source, source + steps) for source in range(initial, last)])


def doc_index(positions, doc_starts):
    return jnp.sum((positions[..., None] >= doc_starts[1:]).astype(jnp.int32), axis=-1)


def allowed_mask(entries, block_index, doc_starts):
    offsets = jnp.arange(BLOCK, dtype=jnp.int32)
    listed = entries >= 0
    clamped = jnp.where(listed, entries, 0)
    query_pos = block_index * BLOCK + offsets
    key_pos = clamped[:, None] * BLOCK + offsets[None, :]
    same_doc = (
        doc_index(key_pos, doc_starts)[None] == doc_index(query_pos, doc_starts)[:, None, None]
    )
    causal = key_pos[None] <= query_pos[:, None, None]
    allowed = listed[None, :, None] & causal & same_doc
    return allowed.reshape(BLOCK, -1)


def softmax_rows(scores, allowed):
    masked = jnp.where(allowed, scores, -1e30)
    row_max = jnp.max(masked, axis=-1, keepdims=True)
    unnormed = jnp.where(allowed, jnp.exp(masked - row_max), 0.0)
    return unnormed / jnp.sum(unnormed, axis=-1, keepdims=True)


def attend_dense(query_blk, grad_blk, key_tiles, value_tiles, allowed, scaling):
    kv_heads, rows_all, width = query_blk.shape
    span = key_tiles.shape[1]
    scores = (
        jnp.einsum("hqd,hkd->hqk", query_blk, key_tiles, preferred_element_type=jnp.float32)
        * scaling
    )
    scores = scores.reshape(kv_heads, rows_all // BLOCK, BLOCK, span)
    attn_probs = softmax_rows(scores, allowed).reshape(kv_heads, rows_all, span)
    probs_low = attn_probs.astype(jnp.bfloat16)
    attended = jnp.einsum(
        "hqk,hkd->hqd", probs_low, value_tiles, preferred_element_type=jnp.float32
    ).astype(jnp.bfloat16)
    row_delta = jnp.einsum("hqd,hqd->hq", grad_blk, attended, preferred_element_type=jnp.float32)
    dprobs = jnp.einsum("hqd,hkd->hqk", grad_blk, value_tiles, preferred_element_type=jnp.float32)
    grad_scores = (attn_probs * (dprobs - row_delta[..., None])).astype(jnp.bfloat16)
    grad_query = (
        jnp.einsum("hqk,hkd->hqd", grad_scores, key_tiles, preferred_element_type=jnp.float32)
        * scaling
    ).astype(jnp.bfloat16)
    grad_key_tiles = (
        jnp.einsum("hqk,hqd->hkd", grad_scores, query_blk, preferred_element_type=jnp.float32)
        * scaling
    )
    grad_value_tiles = jnp.einsum(
        "hqk,hqd->hkd", probs_low, grad_blk, preferred_element_type=jnp.float32
    )
    return (attended, grad_query, grad_key_tiles, grad_value_tiles)


def heads_first(array, heads):
    return jnp.transpose(array.reshape(array.shape[0], heads, HD), (1, 0, 2))


def per_device(queries, keys, values, out_grad, doc_starts, block_lists):
    device = lax.axis_index("ctx")
    blocks = block_lists.shape[0]
    rows_dev = queries.shape[0]
    list_slots = block_lists.shape[1]
    groups = HEADS // KV_HEADS
    scaling = HD ** (-0.5)
    fetched = []
    for distance in range(1, R_DEV + 1):
        fetched.append(shifted((keys, values), "ctx", distance))
    ordered = fetched[::-1] + [(keys, values)]
    key_window = heads_first(
        jnp.concatenate([pair_item[0] for pair_item in ordered], axis=0), KV_HEADS
    )
    value_window = heads_first(
        jnp.concatenate([pair_item[1] for pair_item in ordered], axis=0), KV_HEADS
    )
    window_base = (device - R_DEV) * blocks
    first_block = device * blocks

    def to_blocks(array):
        shaped = array.reshape(blocks, BLOCK, KV_HEADS, groups, HD)
        return jnp.transpose(shaped, (0, 2, 3, 1, 4)).reshape(blocks, KV_HEADS, groups * BLOCK, HD)

    def from_blocks(array):
        shaped = array.reshape(blocks, KV_HEADS, groups, BLOCK, HD)
        return jnp.transpose(shaped, (0, 3, 1, 2, 4)).reshape(rows_dev, HEADS * HD)

    query_blocks = to_blocks(queries)
    grad_blocks = to_blocks(out_grad)

    def per_block(carried, inputs):
        acc_keys, acc_values = carried
        query_blk, grad_blk, entries, block_index = inputs
        listed = entries >= 0
        window_index = jnp.where(listed, entries - window_base, 0)
        key_tiles = jnp.concatenate(
            [
                lax.dynamic_slice_in_dim(key_window, window_index[slot] * BLOCK, BLOCK, 1)
                for slot in range(list_slots)
            ],
            axis=1,
        )
        value_tiles = jnp.concatenate(
            [
                lax.dynamic_slice_in_dim(value_window, window_index[slot] * BLOCK, BLOCK, 1)
                for slot in range(list_slots)
            ],
            axis=1,
        )
        allowed = allowed_mask(entries, block_index, doc_starts)
        attended, grad_query, grad_key_tiles, grad_value_tiles = attend_dense(
            query_blk, grad_blk, key_tiles, value_tiles, allowed, scaling
        )
        for slot in range(list_slots):
            start = window_index[slot] * BLOCK
            old_keys = lax.dynamic_slice_in_dim(acc_keys, start, BLOCK, 1)
            old_values = lax.dynamic_slice_in_dim(acc_values, start, BLOCK, 1)
            acc_keys = lax.dynamic_update_slice_in_dim(
                acc_keys, old_keys + grad_key_tiles[:, slot * BLOCK : (slot + 1) * BLOCK], start, 1
            )
            acc_values = lax.dynamic_update_slice_in_dim(
                acc_values,
                old_values + grad_value_tiles[:, slot * BLOCK : (slot + 1) * BLOCK],
                start,
                1,
            )
        return ((acc_keys, acc_values), (attended, grad_query))

    window_rows = (R_DEV + 1) * rows_dev
    zeros_acc = jnp.zeros((KV_HEADS, window_rows, HD), jnp.float32)
    indices = first_block + jnp.arange(blocks, dtype=jnp.int32)
    (acc_keys, acc_values), (attended, grad_query) = lax.scan(
        per_block, (zeros_acc, zeros_acc), (query_blocks, grad_blocks, block_lists, indices)
    )
    slab_keys = jnp.transpose(acc_keys, (1, 0, 2)).reshape(R_DEV + 1, rows_dev, KV_HEADS * HD)
    slab_values = jnp.transpose(acc_values, (1, 0, 2)).reshape(R_DEV + 1, rows_dev, KV_HEADS * HD)
    summed_keys = slab_keys[R_DEV]
    summed_values = slab_values[R_DEV]
    for distance in range(1, R_DEV + 1):
        returned = shifted(
            (slab_keys[R_DEV - distance], slab_values[R_DEV - distance]), "ctx", -distance
        )
        summed_keys = summed_keys + returned[0]
        summed_values = summed_values + returned[1]
    return (
        from_blocks(attended),
        from_blocks(grad_query),
        summed_keys.astype(jnp.bfloat16),
        summed_values.astype(jnp.bfloat16),
    )


def solution(mesh):
    placed = (
        P(("grp", "ctx"), None),
        P(("grp", "ctx"), None),
        P(("grp", "ctx"), None),
        P(("grp", "ctx"), None),
        P("grp"),
        P(("grp", "ctx"), None),
    )
    return jax.shard_map(
        per_device,
        mesh=mesh,
        in_specs=placed,
        out_specs=(
            P(("grp", "ctx"), None),
            P(("grp", "ctx"), None),
            P(("grp", "ctx"), None),
            P(("grp", "ctx"), None),
        ),
        check_vma=False,
    )
```

profile of v0, /device:TPU:18, one launch (start us, length us, event | category | flops | bytes accessed | tf_op | source)
XLA Modules:
  0.0 329.9 jit_solution(5780523535233906854)
XLA Ops:
  1.9 1.9 collective-permute-start.3
  3.8 3.4 %collective-permute-start.2 = (bf16[512,512]{0,1:T(8,128)(2,1)S(1)}, bf16[512,512]{0,1:T(8,128)(2,1)}, u32[]{:S(2)}, u32[]{:S(2)}) collective-permute-start(bf16[512,512]{0,1:T(8,128)(2,1)S(1)} %copy.49), channel_id=1, source_target_pairs={{0,2},{1,3},{2,4},{3,5},{4,6},{5,7},{6,8},{7,9},{8,10},{9,11},{10,... | collective-permute-start | bytes 1572872 | tf_op jit(solution)/shard_map/ppermute | solution.py:16
  8.5 3.3 collective-permute-start.1
  11.8 3.4 %collective-permute-start = (bf16[512,512]{0,1:T(8,128)(2,1)S(1)}, bf16[512,512]{0,1:T(8,128)(2,1)}, u32[]{:S(2)}, u32[]{:S(2)}) collective-permute-start(bf16[512,512]{0,1:T(8,128)(2,1)S(1)} %copy.45), channel_id=1, source_target_pairs={{0,2},{1,3},{2,4},{3,5},{4,6},{5,7},{6,8},{7,9},{8,10},{9,11},{10,... | collective-permute-start | bytes 1572872 | tf_op jit(solution)/shard_map/ppermute | solution.py:16
  15.2 3.2 reshape.158
  18.5 1.9 copy.44
  20.4 3.2 reshape.161
  23.6 2.0 copy.48
  28.5 7.4 %collective-permute-done.1 = bf16[512,512]{0,1:T(8,128)(2,1)} collective-permute-done((bf16[512,512]{0,1:T(8,128)(2,1)S(1)}, bf16[512,512]{0,1:T(8,128)(2,1)}, u32[]{:S(2)}, u32[]{:S(2)}) %collective-permute-start.1) | collective-permute-done | bytes 524320 | tf_op jit(solution)/shard_map/ppermute | solution.py:16
  39.0 1.9 broadcast_in_dim.43
  40.9 202.9 %while.16 = (s32[]{:T(128)}, f32[4,1536,128]{2,1,0:T(8,128)}, f32[4,1536,128]{2,1,0:T(8,128)S(1)}, bf16[4,4,512,128]{3,2,1,0:T(8,128)(2,1)}, bf16[4,4,512,128]{3...) while((s32[]{:T(128)}, f32[4,1536,128]{2,1,0:T(8,128)}, ...), condition=%wide.region_5.6_spmd, body=%wide.region_0.5_spmd.sunk | while | flops 2436646912 | bytes 115217560 | solution.py:150
  47.4 1.6 dynamic-slice_dynamic-update-slice_fusion.30
  57.0 1.6 dynamic-slice_dynamic-update-slice_fusion.24
  58.6 1.6 dynamic-slice_dynamic-update-slice_fusion.25
  66.6 6.8 %fusion.113 = (f32[4,512]{1,0:T(4,128)S(1)}, f32[4,512,768]{2,1,0:T(8,128)}) fusion(pred[512,768]{1,0:T(8,128)(4,1)S(1)} %bitcast.181, bf16[4,768,128]{2,1,0:T(8,128)(2,1)} %dynamic-slice_dynamic-update-slice_fusion.29, bf16[4,4,512,128]{3,2,1,0:T(8,128)(2,1)} %get-tuple-element.300, s32[]{:T(128)S(6)} %copy.118), kind=kOutput, calls=%fused_computation.110.clone.1 | convolution fusion | flops 410518272 | bytes 8396804 | tf_op jit(solution)/shard_map/while/body/eval_jaxpr/sub | solution.py:40
  73.4 3.4 %fusion.114 = bf16[4,512,768]{2,1,0:T(8,128)(2,1)S(1)} fusion(f32[4,512,768]{2,1,0:T(8,128)} %get-tuple-element.251, f32[4,512]{1,0:T(4,128)S(1)} %get-tuple-element.252), kind=kLoop, calls=%fused_computation.9.clone.1 | loop fusion | flops 3145728 | bytes 9445376 | tf_op jit(solution)/shard_map/while/body/eval_jaxpr/convert_element_type | solution.py:53
  76.8 2.5 fusion.116
  80.6 2.4 multiply_convert_fusion.2
  83.0 2.9 fusion.128
  85.9 2.5 convolution_multiply_fusion.3
  89.9 1.7 copy-done.1
  98.1 1.6 dynamic-slice_dynamic-update-slice_fusion.30
  107.7 1.6 dynamic-slice_dynamic-update-slice_fusion.24
  109.3 1.6 dynamic-slice_dynamic-update-slice_fusion.25
  117.3 6.8 %fusion.113 = (f32[4,512]{1,0:T(4,128)S(1)}, f32[4,512,768]{2,1,0:T(8,128)}) fusion(pred[512,768]{1,0:T(8,128)(4,1)S(1)} %bitcast.181, bf16[4,768,128]{2,1,0:T(8,128)(2,1)} %dynamic-slice_dynamic-update-slice_fusion.29, bf16[4,4,512,128]{3,2,1,0:T(8,128)(2,1)} %get-tuple-element.300, s32[]{:T(128)S(6)} %copy.118), kind=kOutput, calls=%fused_computation.110.clone.1 | convolution fusion | flops 410518272 | bytes 8396804 | tf_op jit(solution)/shard_map/while/body/eval_jaxpr/sub | solution.py:40
  124.1 3.4 %fusion.114 = bf16[4,512,768]{2,1,0:T(8,128)(2,1)S(1)} fusion(f32[4,512,768]{2,1,0:T(8,128)} %get-tuple-element.251, f32[4,512]{1,0:T(4,128)S(1)} %get-tuple-element.252), kind=kLoop, calls=%fused_computation.9.clone.1 | loop fusion | flops 3145728 | bytes 9445376 | tf_op jit(solution)/shard_map/while/body/eval_jaxpr/convert_element_type | solution.py:53
  127.5 2.5 fusion.116
  131.3 2.4 multiply_convert_fusion.2
  133.7 2.9 fusion.128
  136.7 2.5 convolution_multiply_fusion.3
  140.6 1.7 copy-done.1
  148.9 1.6 dynamic-slice_dynamic-update-slice_fusion.30
  158.5 1.6 dynamic-slice_dynamic-update-slice_fusion.24
  160.1 1.6 dynamic-slice_dynamic-update-slice_fusion.25
  168.0 6.8 %fusion.113 = (f32[4,512]{1,0:T(4,128)S(1)}, f32[4,512,768]{2,1,0:T(8,128)}) fusion(pred[512,768]{1,0:T(8,128)(4,1)S(1)} %bitcast.181, bf16[4,768,128]{2,1,0:T(8,128)(2,1)} %dynamic-slice_dynamic-update-slice_fusion.29, bf16[4,4,512,128]{3,2,1,0:T(8,128)(2,1)} %get-tuple-element.300, s32[]{:T(128)S(6)} %copy.118), kind=kOutput, calls=%fused_computation.110.clone.1 | convolution fusion | flops 410518272 | bytes 8396804 | tf_op jit(solution)/shard_map/while/body/eval_jaxpr/sub | solution.py:40
  174.8 3.4 %fusion.114 = bf16[4,512,768]{2,1,0:T(8,128)(2,1)S(1)} fusion(f32[4,512,768]{2,1,0:T(8,128)} %get-tuple-element.251, f32[4,512]{1,0:T(4,128)S(1)} %get-tuple-element.252), kind=kLoop, calls=%fused_computation.9.clone.1 | loop fusion | flops 3145728 | bytes 9445376 | tf_op jit(solution)/shard_map/while/body/eval_jaxpr/convert_element_type | solution.py:53
  178.2 2.5 fusion.116
  182.0 2.4 multiply_convert_fusion.2
  184.4 2.9 fusion.128
  187.4 2.5 convolution_multiply_fusion.3
  191.4 1.7 copy-done.1
  199.6 1.6 dynamic-slice_dynamic-update-slice_fusion.30
  209.2 1.6 dynamic-slice_dynamic-update-slice_fusion.24
  218.7 6.8 %fusion.113 = (f32[4,512]{1,0:T(4,128)S(1)}, f32[4,512,768]{2,1,0:T(8,128)}) fusion(pred[512,768]{1,0:T(8,128)(4,1)S(1)} %bitcast.181, bf16[4,768,128]{2,1,0:T(8,128)(2,1)} %dynamic-slice_dynamic-update-slice_fusion.29, bf16[4,4,512,128]{3,2,1,0:T(8,128)(2,1)} %get-tuple-element.300, s32[]{:T(128)S(6)} %copy.118), kind=kOutput, calls=%fused_computation.110.clone.1 | convolution fusion | flops 410518272 | bytes 8396804 | tf_op jit(solution)/shard_map/while/body/eval_jaxpr/sub | solution.py:40
  225.5 3.4 %fusion.114 = bf16[4,512,768]{2,1,0:T(8,128)(2,1)S(1)} fusion(f32[4,512,768]{2,1,0:T(8,128)} %get-tuple-element.251, f32[4,512]{1,0:T(4,128)S(1)} %get-tuple-element.252), kind=kLoop, calls=%fused_computation.9.clone.1 | loop fusion | flops 3145728 | bytes 9445376 | tf_op jit(solution)/shard_map/while/body/eval_jaxpr/convert_element_type | solution.py:53
  228.9 2.5 fusion.116
  232.7 2.4 multiply_convert_fusion.2
  235.2 2.9 fusion.128
  238.1 2.5 convolution_multiply_fusion.3
  242.1 1.7 copy-done.1
  243.8 3.0 slice_bitcast_fusion.5
  249.1 7.4 %collective-permute-start.4 = (f32[512,512]{1,0:T(8,128)}, f32[512,512]{1,0:T(8,128)}, u32[]{:S(2)}, u32[]{:S(2)}) collective-permute-start(f32[512,512]{1,0:T(8,128)} %bitcast.116), channel_id=1, source_target_pairs={{1,0},{2,1},{3,2},{4,3},{5,4},{6,5},{7,6},{8,7},{9,8},{10,9},{11,1... | collective-permute-start | bytes 3145736 | tf_op jit(solution)/shard_map/ppermute | solution.py:16
  256.6 3.3 %collective-permute-start.5 = (f32[512,512]{1,0:T(8,128)}, f32[512,512]{1,0:T(8,128)}, u32[]{:S(2)}, u32[]{:S(2)}) collective-permute-start(f32[512,512]{1,0:T(8,128)} %bitcast.115), channel_id=1, source_target_pairs={{2,0},{3,1},{4,2},{5,3},{6,4},{7,5},{8,6},{9,7},{10,8},{11,9},{12,... | collective-permute-start | bytes 3145736 | tf_op jit(solution)/shard_map/ppermute | solution.py:16
  263.4 1.9 collective-permute-start.6
  265.3 2.6 collective-permute-start.7
  267.9 1.6 copy.83
  269.6 2.8 reshape.167
  272.4 3.2 copy.84
  275.6 2.8 reshape.165
  279.0 24.4 %collective-permute-done.5 = f32[512,512]{1,0:T(8,128)} collective-permute-done((f32[512,512]{1,0:T(8,128)}, f32[512,512]{1,0:T(8,128)}, u32[]{:S(2)}, u32[]{:S(2)}) %collective-permute-start.5) | collective-permute-done | bytes 1048608 | tf_op jit(solution)/shard_map/ppermute | solution.py:16
  303.5 2.6 fusion.55
  306.0 8.1 %collective-permute-done.6 = f32[512,512]{1,0:T(8,128)} collective-permute-done((f32[512,512]{1,0:T(8,128)}, f32[512,512]{1,0:T(8,128)}, u32[]{:S(2)}, u32[]{:S(2)}) %collective-permute-start.6) | collective-permute-done | bytes 1048608 | tf_op jit(solution)/shard_map/ppermute | solution.py:16
  314.1 13.2 %collective-permute-done.7 = f32[512,512]{1,0:T(8,128)} collective-permute-done((f32[512,512]{1,0:T(8,128)}, f32[512,512]{1,0:T(8,128)}, u32[]{:S(2)}, u32[]{:S(2)}) %collective-permute-start.7) | collective-permute-done | bytes 1048608 | tf_op jit(solution)/shard_map/ppermute | solution.py:16
  327.4 2.6 fusion.53
  (230 shorter events, 93.0 us)
Async XLA Ops:
  1.9 23.7 %collective-permute-start.3 = (bf16[512,512]{0,1:T(8,128)(2,1)S(1)}, bf16[512,512]{0,1:T(8,128)(2,1)}, u32[]{:S(2)}, u32[]{:S(2)}) collective-permute-start(bf16[512,512]{0,1:T(8,128)(2,1)S(1)} %copy.49), channel_id=1, source_target_pairs={{0,1},{1,2},{2,3},{3,4},{4,5},{5,6},{6,7},{7,8},{8,9},{9,10},{10,1... | collective-permute-start | bytes 1572872 | tf_op jit(solution)/shard_map/ppermute | solution.py:16
  3.8 21.8 %collective-permute-start.2 = (bf16[512,512]{0,1:T(8,128)(2,1)S(1)}, bf16[512,512]{0,1:T(8,128)(2,1)}, u32[]{:S(2)}, u32[]{:S(2)}) collective-permute-start(bf16[512,512]{0,1:T(8,128)(2,1)S(1)} %copy.49), channel_id=1, source_target_pairs={{0,2},{1,3},{2,4},{3,5},{4,6},{5,7},{6,8},{7,9},{8,10},{9,11},{10,... | collective-permute-start | bytes 1572872 | tf_op jit(solution)/shard_map/ppermute | solution.py:16
  8.5 27.4 %collective-permute-start.1 = (bf16[512,512]{0,1:T(8,128)(2,1)S(1)}, bf16[512,512]{0,1:T(8,128)(2,1)}, u32[]{:S(2)}, u32[]{:S(2)}) collective-permute-start(bf16[512,512]{0,1:T(8,128)(2,1)S(1)} %copy.45), channel_id=1, source_target_pairs={{0,1},{1,2},{2,3},{3,4},{4,5},{5,6},{6,7},{7,8},{8,9},{9,10},{10,1... | collective-permute-start | bytes 1572872 | tf_op jit(solution)/shard_map/ppermute | solution.py:16
  11.8 24.1 %collective-permute-start = (bf16[512,512]{0,1:T(8,128)(2,1)S(1)}, bf16[512,512]{0,1:T(8,128)(2,1)}, u32[]{:S(2)}, u32[]{:S(2)}) collective-permute-start(bf16[512,512]{0,1:T(8,128)(2,1)S(1)} %copy.45), channel_id=1, source_target_pairs={{0,2},{1,3},{2,4},{3,5},{4,6},{5,7},{6,8},{7,9},{8,10},{9,11},{10,... | collective-permute-start | bytes 1572872 | tf_op jit(solution)/shard_map/ppermute | solution.py:16
  38.8 2.1 copy-start.6
  38.8 2.1 copy-start.7
  40.9 1.5 copy-start.8
  73.4 3.4 %copy-start.2 = (bf16[4,4,512,128]{3,2,1,0:T(8,128)(2,1)S(1)}, bf16[4,4,512,128]{3,2,1,0:T(8,128)(2,1)}, u32[]{:S(2)}) copy-start(bf16[4,4,512,128]{3,2,1,0:T(8,128)(2,1)} %get-tuple-element.302) | copy-start | bytes 6291460 | tf_op jit(solution)/shard_map/while
  73.4 7.2 %slice-start = ((s8[6291456]{0:T(1024)(128)(4,1)}), s8[4194304]{0:T(1024)(128)(4,1)S(1)}, s32[]{:S(2)}) async-start(s8[6291456]{0:T(1024)(128)(4,1)} %bitcast.175), calls=%async_computation | async-start | bytes 8388608 | tf_op jit(solution)/shard_map/while
  76.8 3.8 %slice-start.1 = ((s8[6291456]{0:T(1024)(128)(4,1)}), s8[2097152]{0:T(1024)(128)(4,1)S(1)}, s32[]{:S(2)}) async-start(s8[6291456]{0:T(1024)(128)(4,1)} %bitcast.175), calls=%async_computation.1 | async-start | bytes 4194304 | tf_op jit(solution)/shard_map/while
  85.9 3.3 %copy-start = (f32[4,1536,128]{2,1,0:T(8,128)S(1)}, f32[4,1536,128]{2,1,0:T(8,128)}, u32[]{:S(2)}) copy-start(f32[4,1536,128]{2,1,0:T(8,128)} %get-tuple-element.275) | copy-start | bytes 9437188 | tf_op jit(solution)/shard_map/while
  89.5 2.2 copy-start.9
  89.9 1.7 copy-start.1
  91.6 1.5 copy-start.8
  124.1 3.4 %copy-start.2 = (bf16[4,4,512,128]{3,2,1,0:T(8,128)(2,1)S(1)}, bf16[4,4,512,128]{3,2,1,0:T(8,128)(2,1)}, u32[]{:S(2)}) copy-start(bf16[4,4,512,128]{3,2,1,0:T(8,128)(2,1)} %get-tuple-element.302) | copy-start | bytes 6291460 | tf_op jit(solution)/shard_map/while
  124.1 7.2 %slice-start = ((s8[6291456]{0:T(1024)(128)(4,1)}), s8[4194304]{0:T(1024)(128)(4,1)S(1)}, s32[]{:S(2)}) async-start(s8[6291456]{0:T(1024)(128)(4,1)} %bitcast.175), calls=%async_computation | async-start | bytes 8388608 | tf_op jit(solution)/shard_map/while
  127.5 3.8 %slice-start.1 = ((s8[6291456]{0:T(1024)(128)(4,1)}), s8[2097152]{0:T(1024)(128)(4,1)S(1)}, s32[]{:S(2)}) async-start(s8[6291456]{0:T(1024)(128)(4,1)} %bitcast.175), calls=%async_computation.1 | async-start | bytes 4194304 | tf_op jit(solution)/shard_map/while
  136.7 3.3 %copy-start = (f32[4,1536,128]{2,1,0:T(8,128)S(1)}, f32[4,1536,128]{2,1,0:T(8,128)}, u32[]{:S(2)}) copy-start(f32[4,1536,128]{2,1,0:T(8,128)} %get-tuple-element.275) | copy-start | bytes 9437188 | tf_op jit(solution)/shard_map/while
  140.2 2.2 copy-start.9
  140.6 1.7 copy-start.1
  142.3 1.5 copy-start.8
  174.8 3.4 %copy-start.2 = (bf16[4,4,512,128]{3,2,1,0:T(8,128)(2,1)S(1)}, bf16[4,4,512,128]{3,2,1,0:T(8,128)(2,1)}, u32[]{:S(2)}) copy-start(bf16[4,4,512,128]{3,2,1,0:T(8,128)(2,1)} %get-tuple-element.302) | copy-start | bytes 6291460 | tf_op jit(solution)/shard_map/while
  174.8 7.2 %slice-start = ((s8[6291456]{0:T(1024)(128)(4,1)}), s8[4194304]{0:T(1024)(128)(4,1)S(1)}, s32[]{:S(2)}) async-start(s8[6291456]{0:T(1024)(128)(4,1)} %bitcast.175), calls=%async_computation | async-start | bytes 8388608 | tf_op jit(solution)/shard_map/while
  178.2 3.8 %slice-start.1 = ((s8[6291456]{0:T(1024)(128)(4,1)}), s8[2097152]{0:T(1024)(128)(4,1)S(1)}, s32[]{:S(2)}) async-start(s8[6291456]{0:T(1024)(128)(4,1)} %bitcast.175), calls=%async_computation.1 | async-start | bytes 4194304 | tf_op jit(solution)/shard_map/while
  187.4 3.3 %copy-start = (f32[4,1536,128]{2,1,0:T(8,128)S(1)}, f32[4,1536,128]{2,1,0:T(8,128)}, u32[]{:S(2)}) copy-start(f32[4,1536,128]{2,1,0:T(8,128)} %get-tuple-element.275) | copy-start | bytes 9437188 | tf_op jit(solution)/shard_map/while
  190.9 2.2 copy-start.9
  191.3 1.7 copy-start.1
  193.1 1.5 copy-start.8
  225.5 3.4 %copy-start.2 = (bf16[4,4,512,128]{3,2,1,0:T(8,128)(2,1)S(1)}, bf16[4,4,512,128]{3,2,1,0:T(8,128)(2,1)}, u32[]{:S(2)}) copy-start(bf16[4,4,512,128]{3,2,1,0:T(8,128)(2,1)} %get-tuple-element.302) | copy-start | bytes 6291460 | tf_op jit(solution)/shard_map/while
  225.5 7.2 %slice-start = ((s8[6291456]{0:T(1024)(128)(4,1)}), s8[4194304]{0:T(1024)(128)(4,1)S(1)}, s32[]{:S(2)}) async-start(s8[6291456]{0:T(1024)(128)(4,1)} %bitcast.175), calls=%async_computation | async-start | bytes 8388608 | tf_op jit(solution)/shard_map/while
  228.9 3.8 %slice-start.1 = ((s8[6291456]{0:T(1024)(128)(4,1)}), s8[2097152]{0:T(1024)(128)(4,1)S(1)}, s32[]{:S(2)}) async-start(s8[6291456]{0:T(1024)(128)(4,1)} %bitcast.175), calls=%async_computation.1 | async-start | bytes 4194304 | tf_op jit(solution)/shard_map/while
  238.1 3.3 %copy-start = (f32[4,1536,128]{2,1,0:T(8,128)S(1)}, f32[4,1536,128]{2,1,0:T(8,128)}, u32[]{:S(2)}) copy-start(f32[4,1536,128]{2,1,0:T(8,128)} %get-tuple-element.275) | copy-start | bytes 9437188 | tf_op jit(solution)/shard_map/while
  241.6 2.2 copy-start.9
  242.1 1.7 copy-start.1
  249.1 29.9 %collective-permute-start.4 = (f32[512,512]{1,0:T(8,128)}, f32[512,512]{1,0:T(8,128)}, u32[]{:S(2)}, u32[]{:S(2)}) collective-permute-start(f32[512,512]{1,0:T(8,128)} %bitcast.116), channel_id=1, source_target_pairs={{1,0},{2,1},{3,2},{4,3},{5,4},{6,5},{7,6},{8,7},{9,8},{10,9},{11,1... | collective-permute-start | bytes 3145736 | tf_op jit(solution)/shard_map/ppermute | solution.py:16
  256.6 46.9 %collective-permute-start.5 = (f32[512,512]{1,0:T(8,128)}, f32[512,512]{1,0:T(8,128)}, u32[]{:S(2)}, u32[]{:S(2)}) collective-permute-start(f32[512,512]{1,0:T(8,128)} %bitcast.115), channel_id=1, source_target_pairs={{2,0},{3,1},{4,2},{5,3},{6,4},{7,5},{8,6},{9,7},{10,8},{11,9},{12,... | collective-permute-start | bytes 3145736 | tf_op jit(solution)/shard_map/ppermute | solution.py:16
  261.1 6.8 %copy-start.5 = (bf16[4,4,512,128]{3,2,1,0:T(8,128)(2,1)S(1)}, bf16[4,4,512,128]{3,2,1,0:T(8,128)(2,1)}, u32[]{:S(2)}) copy-start(bf16[4,4,512,128]{3,2,1,0:T(8,128)(2,1)} %get-tuple-element.75) | copy-start | bytes 6291460
  263.4 50.8 %collective-permute-start.6 = (f32[512,512]{1,0:T(8,128)}, f32[512,512]{1,0:T(8,128)}, u32[]{:S(2)}, u32[]{:S(2)}) collective-permute-start(f32[512,512]{1,0:T(8,128)} %bitcast.114), channel_id=1, source_target_pairs={{1,0},{2,1},{3,2},{4,3},{5,4},{6,5},{7,6},{8,7},{9,8},{10,9},{11,1... | collective-permute-start | bytes 3145736 | tf_op jit(solution)/shard_map/ppermute | solution.py:16
  265.3 62.1 %collective-permute-start.7 = (f32[512,512]{1,0:T(8,128)}, f32[512,512]{1,0:T(8,128)}, u32[]{:S(2)}, u32[]{:S(2)}) collective-permute-start(f32[512,512]{1,0:T(8,128)} %bitcast.113), channel_id=1, source_target_pairs={{2,0},{3,1},{4,2},{5,3},{6,4},{7,5},{8,6},{9,7},{10,8},{11,9},{12,... | collective-permute-start | bytes 3145736 | tf_op jit(solution)/shard_map/ppermute | solution.py:16
  275.6 27.9 %copy-start.3 = (f32[4,64,8,128]{3,2,1,0:T(8,128)S(1)}, f32[4,64,8,128]{3,2,1,0:T(8,128)}, u32[]{:S(2)}) copy-start(f32[4,64,8,128]{3,2,1,0:T(8,128)} %get-tuple-element.147) | copy-start | bytes 3145732
  278.4 49.0 %copy-start.4 = (f32[4,64,8,128]{3,2,1,0:T(8,128)S(1)}, f32[4,64,8,128]{3,2,1,0:T(8,128)}, u32[]{:S(2)}) copy-start(f32[4,64,8,128]{3,2,1,0:T(8,128)} %get-tuple-element.144) | copy-start | bytes 3145732
where the time goes:
time: 332 us; the launch traced here: 330 us
  local copies, waits for them, and re-layouts  131 us (39%)
  matrix products  73.4 us (22%)
  waiting for transfers between devices  53.8 us (16%)
  starting transfers between devices  27.3 us (8%)
  other arithmetic  25.3 us (8%)
  loops' own time  18.4 us (6%)
    while x96, local copies, waits for them, and re-layouts  70.8 us
    ppermute x8, waiting for transfers between devices, shifted(): lax.ppermute(value, axis, [(source, source + steps) for source in range(i...  53.8 us
    ppermute x8, starting transfers between devices, shifted(): lax.ppermute(value, axis, [(source, source + steps) for source in range(i...  27.3 us
    sub x4, matrix products, softmax_rows(): unnormed = jnp.where(allowed, jnp.exp(masked - row_max), 0.0)  27.1 us
    another operation x1, loops' own time, per_device(): lax.scan(per_block, (zeros_acc, zeros_acc), (query_blocks, grad_blocks, b...  18.4 us
    convert_element_type x4, other arithmetic, attend_dense(): probs_low = attn_probs.astype(jnp.bfloat16)  13.5 us
    dot_general x4, matrix products, attend_dense(): jnp.einsum('hqk,hkd->hqd', grad_scores, key_tiles, preferred_element_type...  11.7 us
    reshape x4, local copies, waits for them, and re-layouts, to_blocks(): shaped = array.reshape(blocks, BLOCK, KV_HEADS, groups, HD)  10.4 us
  transfers between devices with their start and end apart: 8, of which 5 were waited for; matrix products, arithmetic and copies ran while one was open for 9% of the time, Pallas kernels for 0%

commit v1 on v0

v1 whole, which is shorter than its diff:
```python
import functools

import jax
import jax.numpy as jnp
from jax import lax
from jax.experimental import pallas as pl
from jax.experimental.pallas import tpu as pltpu
from jax.sharding import PartitionSpec as P

HD = 128
BLOCK = 128
R_DEV = 2
MESH = pl.DeviceIdType.MESH
FAR = 1 << 30


def kernel(
    n, blocks, slots, kv_heads, groups,
    index_ref, base_ref, inverse_ref, starts_ref, key_hbm, value_hbm, query_ref, grad_ref,
    out_ref, dquery_ref, dkey_ref, dvalue_ref,
    window, current, turned, bias, parts, own, send_a, send_b, take_a, take_b,
    local_sem, a_send, a_recv, b_send, b_recv, ga_send, ga_recv, gb_send, gb_recv,
):
    me = lax.axis_index("ctx")
    odd = lax.rem(me, 2) == 1
    even = jnp.logical_not(odd)
    partner = me + 1 - 2 * lax.rem(me, 2)
    ahead = lax.rem(me + 2, n)
    behind = lax.rem(me + n - 2, n)
    here = pl.ds(2 * blocks, blocks)
    near = pl.ds(blocks, blocks)
    far = pl.ds(0, blocks)
    span = slots * BLOCK
    scaling = HD ** (-0.5)
    scale2 = scaling * 1.4426950408889634

    def local_copies(g):
        cols = pl.ds(pl.multiple_of(g * HD, HD), HD)
        return [
            pltpu.make_async_copy(
                ref.at[:, :, cols], window.at[g, kind, here], local_sem.at[g, kind]
            )
            for kind, ref in enumerate((key_hbm, value_hbm))
        ]

    def remote(src, dst, send, recv, target):
        return pltpu.make_async_remote_copy(
            src_ref=src, dst_ref=dst, send_sem=send, recv_sem=recv,
            device_id={"ctx": target}, device_id_type=MESH,
        )

    def copy_a(g):
        return remote(
            window.at[g, :, here], window.at[g, :, far], a_send.at[g], a_recv.at[g], ahead
        )

    def copy_b(g, source):
        return remote(
            window.at[g, :, source], window.at[g, :, near], b_send.at[g], b_recv.at[g], partner
        )

    def grad_a(g):
        return remote(send_a.at[g], take_a.at[g], ga_send.at[g], ga_recv.at[g], behind)

    def grad_b(g):
        return remote(send_b.at[g], take_b.at[g], gb_send.at[g], gb_recv.at[g], partner)

    barrier = pltpu.get_barrier_semaphore()
    for other in (ahead, behind, partner):
        pl.semaphore_signal(barrier, inc=1, device_id={"ctx": other}, device_id_type=MESH)
    for g in range(kv_heads):
        for copy in local_copies(g):
            copy.start()
    pl.semaphore_wait(barrier, 3)
    for g in range(kv_heads):
        for copy in local_copies(g):
            copy.wait()
        copy_a(g).start()

        @pl.when(even)
        def _():
            copy_b(g, here).start()

    parts[:, blocks * slots] = jnp.zeros((2, BLOCK, HD), jnp.float32)
    first = me * (blocks * BLOCK)
    lanes = lax.broadcasted_iota(jnp.int32, (1, BLOCK), 1)
    rows = lax.broadcasted_iota(jnp.int32, (BLOCK, BLOCK), 0)
    for b in range(blocks):
        pos = first + b * BLOCK + lanes
        low = jnp.zeros_like(pos)
        for d in range(starts_ref.shape[0]):
            start = starts_ref[d]
            low = jnp.maximum(low, jnp.where(start <= pos, start, 0))
        for s in range(slots):
            at = base_ref[b, s] + rows
            keep = jnp.logical_and(at <= pos, at >= low)
            bias[b, pl.ds(s * BLOCK, BLOCK), :] = jnp.where(keep, 0.0, -1e30)

    def arrive(g):
        copy_a(g).wait_recv()

        @pl.when(odd)
        def _():
            copy_b(g, far).start()

    def forward_grad(g):
        grad_b(g).wait_recv()
        send_a[g] = (
            send_a[g].astype(jnp.float32) + take_b[g].astype(jnp.float32)
        ).astype(jnp.bfloat16)
        grad_a(g).start()

    def attend(g, b):
        cols = pl.ds(pl.multiple_of(g * (groups * HD), groups * HD), groups * HD)
        picks = [index_ref[b, s] for s in range(slots)]
        keys = jnp.concatenate([current[0, w] for w in picks], axis=0)
        values = jnp.concatenate([current[1, w] for w in picks], axis=0)
        keys_t = jnp.concatenate([turned[0, w] for w in picks], axis=1)
        values_t = jnp.concatenate([turned[1, w] for w in picks], axis=1)
        query_all = query_ref[b, :, cols]
        grad_all = grad_ref[b, :, cols]
        mask = jnp.concatenate([bias[b], bias[b]], axis=1)
        dkeys = dvalues = None
        for pair in range(groups // 2):
            tiles = [2 * pair, 2 * pair + 1]
            query = jnp.concatenate([query_all[:, j * HD:(j + 1) * HD] for j in tiles], axis=0)
            grad = jnp.concatenate([grad_all[:, j * HD:(j + 1) * HD] for j in tiles], axis=0)
            nt = (((1,), (1,)), ((), ()))
            scores = lax.dot_general(keys, query, nt, preferred_element_type=jnp.float32)
            dprobs = lax.dot_general(values, grad, nt, preferred_element_type=jnp.float32)
            scores = scores * scale2 + mask
            top = jnp.max(scores, axis=0, keepdims=True)
            probs = jnp.exp2(scores - top)
            probs = probs * (1.0 / jnp.sum(probs, axis=0, keepdims=True))
            low = probs.astype(jnp.bfloat16)
            out_t = jnp.dot(values_t, low, preferred_element_type=jnp.float32).astype(jnp.bfloat16)
            delta = jnp.sum(
                out_t.astype(jnp.float32) * grad.T.astype(jnp.float32), axis=0, keepdims=True
            )
            dscores = (probs * (dprobs - delta)).astype(jnp.bfloat16)
            dquery_t = (
                jnp.dot(keys_t, dscores, preferred_element_type=jnp.float32) * scaling
            ).astype(jnp.bfloat16)
            for at, j in enumerate(tiles):
                spot = pl.ds(pl.multiple_of(g * (groups * HD) + j * HD, HD), HD)
                out_ref[b, :, spot] = out_t[:, at * BLOCK:(at + 1) * BLOCK].T
                dquery_ref[b, :, spot] = dquery_t[:, at * BLOCK:(at + 1) * BLOCK].T
            dkey = jnp.dot(dscores, query, preferred_element_type=jnp.float32)
            dvalue = jnp.dot(low, grad, preferred_element_type=jnp.float32)
            dkeys = dkey if dkeys is None else dkeys + dkey
            dvalues = dvalue if dvalues is None else dvalues + dvalue
        parts[0, pl.ds(b * slots, slots)] = (dkeys * scaling).reshape(slots, BLOCK, HD)
        parts[1, pl.ds(b * slots, slots)] = dvalues.reshape(slots, BLOCK, HD)

    def head(g, _):
        copy_b(g, here).wait_recv()
        for kind in range(2):
            for w in range((R_DEV + 1) * blocks):
                tile = window[g, kind, w]
                current[kind, w] = tile
                turned[kind, w] = tile.T

        def block(b, _):
            @pl.when(jnp.logical_and(b == blocks - 1, g < kv_heads - 1))
            def _():
                arrive(g + 1)

            @pl.when(jnp.logical_and(jnp.logical_and(b == 1, g > 0), odd))
            def _():
                forward_grad(g - 1)

            attend(g, b)
            return 0

        lax.fori_loop(0, blocks, block, 0)
        for kind in range(2):
            for w in range(2 * blocks):
                total = parts[kind, inverse_ref[0, w]]
                for b in range(1, blocks):
                    total = total + parts[kind, inverse_ref[b, w]]
                into, at = (send_a, w) if w < blocks else (send_b, w - blocks)
                into[g, kind, at] = total.astype(jnp.bfloat16)
        grad_b(g).start()

        @pl.when(even)
        def _():
            grad_a(g).start()

        for kind in range(2):
            for j in range(blocks):
                total = parts[kind, j * slots]
                for b in range(j + 1, blocks):
                    total = total + parts[kind, inverse_ref[b, 2 * blocks + j]]
                own[g, kind, j] = total
        return 0

    arrive(0)
    lax.fori_loop(0, kv_heads, head, 0)

    @pl.when(odd)
    def _():
        forward_grad(kv_heads - 1)

    for g in range(kv_heads):
        @pl.when(even)
        def _():
            grad_b(g).wait_recv()
            own[g] = own[g] + take_b[g].astype(jnp.float32)

        grad_a(g).wait_recv()
        cols = pl.ds(g * HD, HD)
        for kind, ref in enumerate((dkey_ref, dvalue_ref)):
            ref[:, :, cols] = (own[g, kind] + take_a[g, kind].astype(jnp.float32)).astype(
                jnp.bfloat16
            )
    for g in range(kv_heads):
        copy_a(g).wait_send()

        @pl.when(even)
        def _():
            copy_b(g, here).wait_send()

        @pl.when(odd)
        def _():
            copy_b(g, far).wait_send()

        grad_a(g).wait_send()
        grad_b(g).wait_send()


def per_device(n, queries, keys, values, out_grad, doc_starts, block_lists):
    device = lax.axis_index("ctx")
    blocks, slots = block_lists.shape
    rows = queries.shape[0]
    kv_heads = keys.shape[1] // HD
    groups = queries.shape[1] // keys.shape[1]
    window_blocks = (R_DEV + 1) * blocks
    listed = block_lists >= 0
    at = block_lists - (device - R_DEV) * blocks
    index = jnp.where(listed, at, R_DEV * blocks)
    base = jnp.where(listed, block_lists * BLOCK, FAR)
    hit = (at[:, :, None] == jnp.arange(window_blocks)[None, None, :]) & listed[:, :, None]
    place = jnp.arange(blocks)[:, None, None] * slots + jnp.arange(slots)[None, :, None]
    inverse = jnp.min(jnp.where(hit, place, blocks * slots), axis=1).astype(jnp.int32)
    wide, slim = queries.shape[1], keys.shape[1]

    def shaped(array):
        return array.reshape(blocks, BLOCK, array.shape[1])

    smem = pl.BlockSpec(memory_space=pltpu.SMEM)
    vmem = pl.BlockSpec(memory_space=pltpu.VMEM)
    hbm = pl.BlockSpec(memory_space=pl.ANY)
    bf16, f32 = jnp.bfloat16, jnp.float32
    chunk = (kv_heads, 2, blocks, BLOCK, HD)
    dma = pltpu.SemaphoreType.DMA
    results = pl.pallas_call(
        functools.partial(kernel, n, blocks, slots, kv_heads, groups),
        out_shape=(
            jax.ShapeDtypeStruct((blocks, BLOCK, wide), bf16),
            jax.ShapeDtypeStruct((blocks, BLOCK, wide), bf16),
            jax.ShapeDtypeStruct((blocks, BLOCK, slim), bf16),
            jax.ShapeDtypeStruct((blocks, BLOCK, slim), bf16),
        ),
        in_specs=[smem] * 4 + [hbm] * 2 + [vmem] * 2,
        out_specs=[vmem] * 4,
        scratch_shapes=[
            pltpu.VMEM((kv_heads, 2, window_blocks, BLOCK, HD), bf16),
            pltpu.VMEM((2, window_blocks, BLOCK, HD), bf16),
            pltpu.VMEM((2, window_blocks, BLOCK, HD), bf16),
            pltpu.VMEM((blocks, slots * BLOCK, BLOCK), f32),
            pltpu.VMEM((2, blocks * slots + 1, BLOCK, HD), f32),
            pltpu.VMEM(chunk, f32),
            pltpu.VMEM(chunk, bf16),
            pltpu.VMEM(chunk, bf16),
            pltpu.VMEM(chunk, bf16),
            pltpu.VMEM(chunk, bf16),
            dma((kv_heads, 2)),
        ] + [dma((kv_heads,))] * 8,
        compiler_params=pltpu.CompilerParams(
            collective_id=0, has_side_effects=True, vmem_limit_bytes=56 * 1024 * 1024
        ),
        cost_estimate=pl.CostEstimate(
            flops=12 * rows * wide * slots * BLOCK,
            bytes_accessed=8 * rows * (wide + slim),
            transcendentals=rows * (wide // HD) * slots * BLOCK,
        ),
    )(
        index.astype(jnp.int32), base.astype(jnp.int32), inverse, doc_starts,
        shaped(keys), shaped(values), shaped(queries), shaped(out_grad),
    )
    return tuple(result.reshape(rows, result.shape[2]) for result in results)


def solution(mesh):
    both = P(("grp", "ctx"), None)
    return jax.shard_map(
        functools.partial(per_device, mesh.shape["ctx"]),
        mesh=mesh,
        in_specs=(both, both, both, both, P("grp"), both),
        out_specs=(both, both, both, both),
        check_vma=False,
    )
```

time: 332 us -> 75.9 us (0.23)
  the two profiles are of different devices: /device:TPU:18 before, /device:TPU:1 now
where the time goes in v1:
time: 75.9 us; the launch traced here: 75.7 us
  Pallas kernels  65.4 us (86%)
  local copies, waits for them, and re-layouts  6.47 us (9%)
  other arithmetic  3.21 us (4%)
    pallas_call x1, Pallas kernels, per_device(): pl.pallas_call(functools.partial(kernel, n, blocks, slots, kv_heads, grou...  65.4 us
    unnamed x10, local copies, waits for them, and re-layouts  6.27 us

profile of v1, /device:TPU:1, one launch (start us, length us, event | category | flops | bytes accessed | tf_op | source)
XLA Modules:
  0.0 75.7 jit_solution(1726345630755412159)
XLA Ops:
  0.6 1.3 %multiply_select_fusion = (s32[4,6]{1,0:T(4,128)}, pred[4,6]{1,0:T(4,128)(4,1)S(1)}) fusion(s32[4,6]{1,0:T(4,128)} %param.11), kind=kLoop, calls=%fused_computation.4 | loop fusion | flops 72 | bytes 216 | tf_op jit(solution)/shard_map/jit(_where)/select_n | solution.py:241
  1.9 0.1 copy.11
  2.0 1.3 %broadcast_select_fusion = (s32[4,6]{1,0:T(4,128)}, s32[4,6]{1,0:T(4,128)S(1)}) fusion(pred[4,6]{1,0:T(4,128)(4,1)S(1)} %get-tuple-element.13, s32[4,6]{1,0:T(4,128)} %param.11, s32[]{:T(128)S(6)} %mul.14), kind=kLoop, calls=%fused_computation.5 | loop fusion | flops 48 | bytes 316 | tf_op jit(solution)/shard_map/jit(_where)/select_n | solution.py:240
  3.3 0.1 copy.10
  3.4 0.7 select_reduce_fusion.inverse_ref
  4.1 65.4 %shard_map.93 = (bf16[4,128,2048]{2,1,0:T(8,128)(2,1)}, bf16[4,128,2048]{2,1,0:T(8,128)(2,1)}, bf16[4,128,512]{2,1,0:T(8,128)(2,1)}, bf16[4,128,512]{2,1,0:T(8,128)(2,1)}) custom-call(s32[4,6]{1,0:T(4,128)} %get-tuple-element.14.index_ref, s32[4,6]{1,0:T(4,128)} %get-tuple-element.12.base_ref, s32[4,12]{1,0:T(4,128)} %select_reduce_fusion.inverse_ref, ...), custom_call_target="tpu_custom_call" | custom-call | flops 9663676416 | bytes 10485760 | tf_op jit(solution)/shard_map/pallas_call | solution.py:256
  69.4 0.0 copy-start
  69.5 3.3 %copy.16 = bf16[512,2048]{1,0:T(8,128)(2,1)} copy(bf16[512,2048]{1,0:T(8,128)(2,1)} %bitcast.9) | data formatting | bytes 4194304
  72.8 0.0 copy-done
  72.8 0.0 copy-start.2
  72.8 0.0 copy-start.1
  72.8 1.3 %copy.17 = bf16[512,2048]{1,0:T(8,128)(2,1)} copy(bf16[512,2048]{1,0:T(8,128)(2,1)S(1)} %bitcast.8) | data formatting | bytes 4194304
  74.1 0.1 copy-done.2
  74.1 0.8 %copy.18 = bf16[512,512]{1,0:T(8,128)(2,1)} copy(bf16[512,512]{1,0:T(8,128)(2,1)S(1)} %bitcast.11) | data formatting | bytes 1048576
  74.9 0.0 copy-done.1
  74.9 0.8 %copy.19 = bf16[512,512]{1,0:T(8,128)(2,1)} copy(bf16[512,512]{1,0:T(8,128)(2,1)S(1)} %bitcast.10) | data formatting | bytes 1048576
  (2 shorter events, 0.0 us)
Async XLA Ops:
  69.4 3.3 %copy-start = (bf16[4,128,2048]{2,1,0:T(8,128)(2,1)S(1)}, bf16[4,128,2048]{2,1,0:T(8,128)(2,1)}, u32[]{:S(2)}) copy-start(bf16[4,128,2048]{2,1,0:T(8,128)(2,1)} %get-tuple-element.9) | copy-start | bytes 6291460
  72.8 1.4 %copy-start.2 = (bf16[4,128,512]{2,1,0:T(8,128)(2,1)S(1)}, bf16[4,128,512]{2,1,0:T(8,128)(2,1)}, u32[]{:S(2)}) copy-start(bf16[4,128,512]{2,1,0:T(8,128)(2,1)} %get-tuple-element.10) | copy-start | bytes 1572868
  72.8 2.2 %copy-start.1 = (bf16[4,128,512]{2,1,0:T(8,128)(2,1)S(1)}, bf16[4,128,512]{2,1,0:T(8,128)(2,1)}, u32[]{:S(2)}) copy-start(bf16[4,128,512]{2,1,0:T(8,128)(2,1)} %get-tuple-element.11) | copy-start | bytes 1572868

commit v2 on v1

v2 whole, which is shorter than its diff:
```python
import functools

import jax
import jax.numpy as jnp
from jax import lax
from jax.experimental import pallas as pl
from jax.experimental.pallas import tpu as pltpu
from jax.sharding import PartitionSpec as P

HD = 128
BLOCK = 128
R_DEV = 2
MESH = pl.DeviceIdType.MESH
FAR = 1 << 30


def kernel(
    n, blocks, slots, kv_heads, groups,
    lists_ref, starts_ref, key_hbm, value_hbm, query_hbm, grad_hbm,
    out_hbm, dquery_hbm, dkey_ref, dvalue_ref,
    window, current, turned, bias, parts, own, send_a, send_b, take_a, take_b,
    query_buf, grad_buf, out_buf, dquery_buf, inverse,
    local_sem, load_sem, store_sem,
    a_send, a_recv, b_send, b_recv, ga_send, ga_recv, gb_send, gb_recv,
):
    me = lax.axis_index("ctx")
    odd = lax.rem(me, 2) == 1
    even = jnp.logical_not(odd)
    partner = me + 1 - 2 * lax.rem(me, 2)
    ahead = lax.rem(me + 2, n)
    behind = lax.rem(me + n - 2, n)
    here = pl.ds(2 * blocks, blocks)
    near = pl.ds(blocks, blocks)
    far = pl.ds(0, blocks)
    wide = groups * HD
    scaling = HD ** (-0.5)
    scale2 = scaling * 1.4426950408889634
    window_base = (me - R_DEV) * blocks

    def local_copies(g):
        cols = pl.ds(pl.multiple_of(g * HD, HD), HD)
        return [
            pltpu.make_async_copy(
                ref.at[:, :, cols], window.at[g, kind, here], local_sem.at[g, kind]
            )
            for kind, ref in enumerate((key_hbm, value_hbm))
        ]

    def loads(g):
        cols = pl.ds(pl.multiple_of(g * wide, wide), wide)
        return [
            pltpu.make_async_copy(ref.at[:, :, cols], buf.at[:, :, cols], load_sem.at[g, kind])
            for kind, (ref, buf) in enumerate(((query_hbm, query_buf), (grad_hbm, grad_buf)))
        ]

    def stores(g):
        cols = pl.ds(pl.multiple_of(g * wide, wide), wide)
        return [
            pltpu.make_async_copy(buf.at[:, :, cols], ref.at[:, :, cols], store_sem.at[g, kind])
            for kind, (ref, buf) in enumerate(((out_hbm, out_buf), (dquery_hbm, dquery_buf)))
        ]

    def remote(src, dst, send, recv, target):
        return pltpu.make_async_remote_copy(
            src_ref=src, dst_ref=dst, send_sem=send, recv_sem=recv,
            device_id={"ctx": target}, device_id_type=MESH,
        )

    def copy_a(g):
        return remote(
            window.at[g, :, here], window.at[g, :, far], a_send.at[g], a_recv.at[g], ahead
        )

    def copy_b(g, source):
        return remote(
            window.at[g, :, source], window.at[g, :, near], b_send.at[g], b_recv.at[g], partner
        )

    def grad_a(g):
        return remote(send_a.at[g], take_a.at[g], ga_send.at[g], ga_recv.at[g], behind)

    def grad_b(g):
        return remote(send_b.at[g], take_b.at[g], gb_send.at[g], gb_recv.at[g], partner)

    barrier = pltpu.get_barrier_semaphore()
    for other in (ahead, behind, partner):
        pl.semaphore_signal(barrier, inc=1, device_id={"ctx": other}, device_id_type=MESH)
    for g in range(kv_heads):
        for copy in local_copies(g):
            copy.start()
    for g in range(kv_heads):
        for copy in loads(g):
            copy.start()
    pl.semaphore_wait(barrier, 3)
    for g in range(kv_heads):
        for copy in local_copies(g):
            copy.wait()
        if g == 0:
            copy_a(g).start()

        @pl.when(even)
        def _():
            copy_b(g, here).start()

    parts[:, blocks * slots] = jnp.zeros((2, BLOCK, HD), jnp.float32)
    for b in range(blocks):
        for w in range((R_DEV + 1) * blocks):
            found = jnp.int32(blocks * slots)
            for s in range(slots):
                found = jnp.where(lists_ref[b, s] == window_base + w, b * slots + s, found)
            inverse[b, w] = jnp.where(window_base + w >= 0, found, blocks * slots)
    first = me * (blocks * BLOCK)
    lanes = lax.broadcasted_iota(jnp.int32, (1, BLOCK), 1)
    rows = lax.broadcasted_iota(jnp.int32, (BLOCK, BLOCK), 0)
    for b in range(blocks):
        pos = first + b * BLOCK + lanes
        low = jnp.zeros_like(pos)
        for d in range(starts_ref.shape[0]):
            start = starts_ref[d]
            low = jnp.maximum(low, jnp.where(start <= pos, start, 0))
        for s in range(slots):
            entry = lists_ref[b, s]
            at = jnp.where(entry >= 0, entry * BLOCK, FAR) + rows
            keep = jnp.logical_and(at <= pos, at >= low)
            bias[b, pl.ds(s * BLOCK, BLOCK), :] = jnp.where(keep, 0.0, -1e30).astype(jnp.bfloat16)
    copy_a(0).wait_send()
    copy_a(1).start()

    def arrive(g):
        copy_a(g).wait_recv()

        @pl.when(odd)
        def _():
            copy_b(g, far).start()

    def forward_grad(g):
        grad_b(g).wait_recv()
        send_a[g] = (
            send_a[g].astype(jnp.float32) + take_b[g].astype(jnp.float32)
        ).astype(jnp.bfloat16)
        grad_a(g).start()

    nt = (((1,), (1,)), ((), ()))
    square = lax.broadcasted_iota(jnp.int32, (BLOCK, BLOCK), 1) == rows
    one_hot = jnp.where(square, 1.0, 0.0).astype(jnp.bfloat16)
    one_hot = jnp.concatenate([one_hot, one_hot], axis=0)

    def attend(g, half):
        pairs = groups // 2
        chains = [(at, pair) for at in range(blocks // 2) for pair in range(pairs)]

        def place(at):
            return half * (blocks // 2) + at

        def picks(at):
            found = []
            for s in range(slots):
                entry = lists_ref[place(at), s]
                spot = jnp.where(entry >= 0, entry - window_base, R_DEV * blocks)
                found.append(jnp.clip(spot, 0, (R_DEV + 1) * blocks - 1))
            return found

        tiles = {}

        def score(chain):
            at, pair = chain
            b = place(at)
            if at not in tiles:
                found = picks(at)
                keys = jnp.concatenate([current[0, w] for w in found], axis=0)
                tiles[at] = (found, jnp.concatenate([keys, bias[b]], axis=1))
            spot = pl.ds(pl.multiple_of(g * wide + pair * 2 * HD, 2 * HD), 2 * HD)
            query_two = query_buf[b, :, spot]
            query = jnp.concatenate([query_two[:, :HD], query_two[:, HD:]], axis=0)
            deep = jnp.concatenate([query, one_hot], axis=1)
            return query, lax.dot_general(
                tiles[at][1], deep, nt, preferred_element_type=jnp.float32
            )

        sums = {}

        def rest(chain, query, scores):
            at, pair = chain
            b = place(at)
            found = tiles[at][0]
            spot = pl.ds(pl.multiple_of(g * wide + pair * 2 * HD, 2 * HD), 2 * HD)
            grad_two = grad_buf[b, :, spot]
            grad_t = jnp.concatenate([grad_two[:, :HD].T, grad_two[:, HD:].T], axis=1)
            values = jnp.concatenate([current[1, w] for w in found], axis=0)
            keys_t = jnp.concatenate([turned[0, w] for w in found], axis=1)
            values_t = jnp.concatenate([turned[1, w] for w in found], axis=1)
            top = jnp.max(scores, axis=0, keepdims=True) * scale2
            probs = jnp.exp2(scores * scale2 - top)
            inv = 1.0 / jnp.sum(probs, axis=0, keepdims=True)
            grad_t = (grad_t.astype(jnp.float32) * inv).astype(jnp.bfloat16)
            dprobs = jnp.dot(values, grad_t, preferred_element_type=jnp.float32)
            low = probs.astype(jnp.bfloat16)
            out_t = jnp.dot(values_t, low, preferred_element_type=jnp.float32)
            out_t = (out_t * inv).astype(jnp.bfloat16)
            delta = jnp.sum(
                out_t.astype(jnp.float32) * grad_t.astype(jnp.float32), axis=0, keepdims=True
            )
            dscores = (probs * (dprobs - delta)).astype(jnp.bfloat16)
            dvalue = lax.dot_general(low, grad_t, nt, preferred_element_type=jnp.float32)
            dquery_t = (
                jnp.dot(keys_t, dscores, preferred_element_type=jnp.float32) * scaling
            ).astype(jnp.bfloat16)
            dkey = jnp.dot(dscores, query, preferred_element_type=jnp.float32)
            out_buf[b, :, spot] = jnp.concatenate([out_t[:, :BLOCK].T, out_t[:, BLOCK:].T], axis=1)
            dquery_buf[b, :, spot] = jnp.concatenate(
                [dquery_t[:, :BLOCK].T, dquery_t[:, BLOCK:].T], axis=1
            )
            if pair == 0:
                sums[at] = (dkey, dvalue)
            else:
                sums[at] = (sums[at][0] + dkey, sums[at][1] + dvalue)
            if pair == pairs - 1:
                kept = pl.ds(b * slots, slots)
                parts[0, kept] = (sums[at][0] * scaling).reshape(slots, BLOCK, HD)
                parts[1, kept] = sums[at][1].reshape(slots, BLOCK, HD)

        ready = score(chains[0])
        for i, chain in enumerate(chains):
            now = ready
            if i + 1 < len(chains):
                ready = score(chains[i + 1])
            rest(chain, *now)

    def head(g, _):
        copy_b(g, here).wait_recv()
        for copy in loads(g):
            copy.wait()
        for kind in range(2):
            for w in range((R_DEV + 1) * blocks):
                tile = window[g, kind, w]
                current[kind, w] = tile
                turned[kind, w] = tile.T

        def block(half, _):
            @pl.when(half == 1)
            def _():
                @pl.when(g < kv_heads - 2)
                def _():
                    copy_a(g + 1).wait_send()
                    copy_a(g + 2).start()

                @pl.when(g < kv_heads - 1)
                def _():
                    arrive(g + 1)

                @pl.when(jnp.logical_and(g > 0, odd))
                def _():
                    forward_grad(g - 1)

            attend(g, half)
            return 0

        lax.fori_loop(0, 2, block, 0)
        for kind in range(2):
            for w in range(blocks, 2 * blocks):
                total = parts[kind, inverse[0, w]]
                for b in range(1, blocks):
                    total = total + parts[kind, inverse[b, w]]
                send_b[g, kind, w - blocks] = total.astype(jnp.bfloat16)
        grad_b(g).start()
        for kind in range(2):
            for w in range(blocks):
                total = parts[kind, inverse[0, w]]
                for b in range(1, blocks):
                    total = total + parts[kind, inverse[b, w]]
                send_a[g, kind, w] = total.astype(jnp.bfloat16)

        @pl.when(even)
        def _():
            grad_a(g).start()

        for copy in stores(g):
            copy.start()
        for kind in range(2):
            for j in range(blocks):
                total = parts[kind, j * slots]
                for b in range(j + 1, blocks):
                    total = total + parts[kind, inverse[b, 2 * blocks + j]]
                own[g, kind, j] = total
        return 0

    arrive(0)
    lax.fori_loop(0, kv_heads, head, 0)

    @pl.when(odd)
    def _():
        forward_grad(kv_heads - 1)

    for g in range(kv_heads):
        @pl.when(even)
        def _():
            grad_b(g).wait_recv()
            own[g] = own[g] + take_b[g].astype(jnp.float32)

        grad_a(g).wait_recv()
        cols = pl.ds(g * HD, HD)
        for kind, ref in enumerate((dkey_ref, dvalue_ref)):
            ref[:, :, cols] = (own[g, kind] + take_a[g, kind].astype(jnp.float32)).astype(
                jnp.bfloat16
            )
    copy_a(kv_heads - 1).wait_send()
    for g in range(kv_heads):
        @pl.when(even)
        def _():
            copy_b(g, here).wait_send()

        @pl.when(odd)
        def _():
            copy_b(g, far).wait_send()

        grad_a(g).wait_send()
        grad_b(g).wait_send()
        for copy in stores(g):
            copy.wait()


def per_device(n, queries, keys, values, out_grad, doc_starts, block_lists):
    blocks, slots = block_lists.shape
    rows = queries.shape[0]
    kv_heads = keys.shape[1] // HD
    groups = queries.shape[1] // keys.shape[1]
    window_blocks = (R_DEV + 1) * blocks
    wide, slim = queries.shape[1], keys.shape[1]

    def shaped(array):
        return array.reshape(blocks, BLOCK, array.shape[1])

    smem = pl.BlockSpec(memory_space=pltpu.SMEM)
    vmem = pl.BlockSpec(memory_space=pltpu.VMEM)
    hbm = pl.BlockSpec(memory_space=pl.ANY)
    bf16, f32 = jnp.bfloat16, jnp.float32
    chunk = (kv_heads, 2, blocks, BLOCK, HD)
    dma = pltpu.SemaphoreType.DMA
    results = pl.pallas_call(
        functools.partial(kernel, n, blocks, slots, kv_heads, groups),
        out_shape=(
            jax.ShapeDtypeStruct((blocks, BLOCK, wide), bf16),
            jax.ShapeDtypeStruct((blocks, BLOCK, wide), bf16),
            jax.ShapeDtypeStruct((blocks, BLOCK, slim), bf16),
            jax.ShapeDtypeStruct((blocks, BLOCK, slim), bf16),
        ),
        in_specs=[smem] * 2 + [hbm] * 4,
        out_specs=[hbm] * 2 + [vmem] * 2,
        scratch_shapes=[
            pltpu.VMEM((kv_heads, 2, window_blocks, BLOCK, HD), bf16),
            pltpu.VMEM((2, window_blocks, BLOCK, HD), bf16),
            pltpu.VMEM((2, window_blocks, BLOCK, HD), bf16),
            pltpu.VMEM((blocks, slots * BLOCK, BLOCK), bf16),
            pltpu.VMEM((2, blocks * slots + 1, BLOCK, HD), f32),
            pltpu.VMEM(chunk, f32),
            pltpu.VMEM(chunk, bf16),
            pltpu.VMEM(chunk, bf16),
            pltpu.VMEM(chunk, bf16),
            pltpu.VMEM(chunk, bf16),
        ] + [pltpu.VMEM((blocks, BLOCK, wide), bf16)] * 4 + [
            pltpu.SMEM((blocks, window_blocks), jnp.int32),
        ] + [dma((kv_heads, 2))] * 3 + [dma((kv_heads,))] * 8,
        compiler_params=pltpu.CompilerParams(
            collective_id=0, has_side_effects=True, vmem_limit_bytes=56 * 1024 * 1024
        ),
        cost_estimate=pl.CostEstimate(
            flops=12 * rows * wide * slots * BLOCK,
            bytes_accessed=8 * rows * (wide + slim),
            transcendentals=rows * (wide // HD) * slots * BLOCK,
        ),
    )(
        block_lists, doc_starts, shaped(keys), shaped(values), shaped(queries), shaped(out_grad),
    )
    return tuple(result.reshape(rows, result.shape[2]) for result in results)


def solution(mesh):
    both = P(("grp", "ctx"), None)
    return jax.shard_map(
        functools.partial(per_device, mesh.shape["ctx"]),
        mesh=mesh,
        in_specs=(both, both, both, both, P("grp"), both),
        out_specs=(both, both, both, both),
        check_vma=False,
    )
```

time: 75.9 us -> 74.9 us (0.987)
  other arithmetic: 3.21 us -> 0 us
  Pallas kernels: 65.4 us -> 67.8 us
    select_n x2 -> x0, other arithmetic: 2.53 us -> none  [the longest x1 1.26 us: per_device(): base = jnp.where(listed, block_lists * BLOCK, FAR)]
    pallas_call x1, Pallas kernels: 65.4 us -> 67.8 us  [per_device(): pl.pallas_call(functools.partial(kernel, n, blocks, slots, kv_heads, grou...]
where the time goes in v2:
time: 74.9 us; the launch traced here: 74.7 us
  Pallas kernels  67.8 us (91%)
  local copies, waits for them, and re-layouts  6.27 us (8%)
    pallas_call x1, Pallas kernels, per_device(): pl.pallas_call(functools.partial(kernel, n, blocks, slots, kv_heads, grou...  67.8 us
    unnamed x10, local copies, waits for them, and re-layouts  6.27 us

profile of v2, /device:TPU:1, one launch (start us, length us, event | category | flops | bytes accessed | tf_op | source)
XLA Modules:
  0.0 74.7 jit_solution(13350162175028474856)
XLA Ops:
  0.6 67.8 %shard_map.93 = (bf16[4,128,2048]{2,1,0:T(8,128)(2,1)}, bf16[4,128,2048]{2,1,0:T(8,128)(2,1)}, bf16[4,128,512]{2,1,0:T(8,128)(2,1)}, bf16[4,128,512]{2,1,0:T(8,128)(2,1)}) custom-call(s32[4,6]{1,0:T(4,128)} %lists_ref.1, s32[8]{0:T(128)} %starts_ref.1, bf16[4,128,512]{2,1,0:T(8,128)(2,1)} %bitcast.14, bf16[4,128,512]{2,1,0:T(8,128)(2,1)} %bitcast.15, ...), custom_call_target="tpu_custom_call" | custom-call | flops 9663676416 | bytes 10485760 | tf_op jit(solution)/shard_map/pallas_call | solution.py:339
  68.4 0.0 copy-start
  68.4 3.3 %copy.14 = bf16[512,2048]{1,0:T(8,128)(2,1)} copy(bf16[512,2048]{1,0:T(8,128)(2,1)} %bitcast.9) | data formatting | bytes 4194304
  71.7 0.0 copy-done
  71.7 0.0 copy-start.2
  71.7 0.0 copy-start.1
  71.7 1.3 %copy.15 = bf16[512,2048]{1,0:T(8,128)(2,1)} copy(bf16[512,2048]{1,0:T(8,128)(2,1)S(1)} %bitcast.8) | data formatting | bytes 4194304
  73.0 0.1 copy-done.2
  73.1 0.8 %copy.16 = bf16[512,512]{1,0:T(8,128)(2,1)} copy(bf16[512,512]{1,0:T(8,128)(2,1)S(1)} %bitcast.11) | data formatting | bytes 1048576
  73.9 0.0 copy-done.1
  73.9 0.8 %copy.17 = bf16[512,512]{1,0:T(8,128)(2,1)} copy(bf16[512,512]{1,0:T(8,128)(2,1)S(1)} %bitcast.10) | data formatting | bytes 1048576
Async XLA Ops:
  68.4 3.3 %copy-start = (bf16[4,128,2048]{2,1,0:T(8,128)(2,1)S(1)}, bf16[4,128,2048]{2,1,0:T(8,128)(2,1)}, u32[]{:S(2)}) copy-start(bf16[4,128,2048]{2,1,0:T(8,128)(2,1)} %get-tuple-element.9) | copy-start | bytes 6291460
  71.7 1.4 %copy-start.2 = (bf16[4,128,512]{2,1,0:T(8,128)(2,1)S(1)}, bf16[4,128,512]{2,1,0:T(8,128)(2,1)}, u32[]{:S(2)}) copy-start(bf16[4,128,512]{2,1,0:T(8,128)(2,1)} %get-tuple-element.10) | copy-start | bytes 1572868
  71.7 2.2 %copy-start.1 = (bf16[4,128,512]{2,1,0:T(8,128)(2,1)S(1)}, bf16[4,128,512]{2,1,0:T(8,128)(2,1)}, u32[]{:S(2)}) copy-start(bf16[4,128,512]{2,1,0:T(8,128)(2,1)} %get-tuple-element.11) | copy-start | bytes 1572868

commit v3 on v1

--- a/solution.py
+++ b/solution.py
@@ -16,10 +16,12 @@
 
 def kernel(
     n, blocks, slots, kv_heads, groups,
-    index_ref, base_ref, inverse_ref, starts_ref, key_hbm, value_hbm, query_ref, grad_ref,
-    out_ref, dquery_ref, dkey_ref, dvalue_ref,
+    lists_ref, starts_ref, key_hbm, value_hbm, query_hbm, grad_hbm,
+    out_hbm, dquery_hbm, dkey_ref, dvalue_ref,
     window, current, turned, bias, parts, own, send_a, send_b, take_a, take_b,
-    local_sem, a_send, a_recv, b_send, b_recv, ga_send, ga_recv, gb_send, gb_recv,
+    query_buf, grad_buf, out_buf, dquery_buf, inverse,
+    local_sem, load_sem, store_sem,
+    a_send, a_recv, b_send, b_recv, ga_send, ga_recv, gb_send, gb_recv,
 ):
     me = lax.axis_index("ctx")
     odd = lax.rem(me, 2) == 1
@@ -30,9 +32,10 @@
     here = pl.ds(2 * blocks, blocks)
     near = pl.ds(blocks, blocks)
     far = pl.ds(0, blocks)
-    span = slots * BLOCK
+    wide = groups * HD
     scaling = HD ** (-0.5)
     scale2 = scaling * 1.4426950408889634
+    window_base = (me - R_DEV) * blocks
 
     def local_copies(g):
         cols = pl.ds(pl.multiple_of(g * HD, HD), HD)
@@ -43,6 +46,20 @@
             for kind, ref in enumerate((key_hbm, value_hbm))
         ]
 
+    def loads(g):
+        cols = pl.ds(pl.multiple_of(g * wide, wide), wide)
+        return [
+            pltpu.make_async_copy(ref.at[:, :, cols], buf.at[:, :, cols], load_sem.at[g, kind])
+            for kind, (ref, buf) in enumerate(((query_hbm, query_buf), (grad_hbm, grad_buf)))
+        ]
+
+    def stores(g):
+        cols = pl.ds(pl.multiple_of(g * wide, wide), wide)
+        return [
+            pltpu.make_async_copy(buf.at[:, :, cols], ref.at[:, :, cols], store_sem.at[g, kind])
+            for kind, (ref, buf) in enumerate(((out_hbm, out_buf), (dquery_hbm, dquery_buf)))
+        ]
+
     def remote(src, dst, send, recv, target):
         return pltpu.make_async_remote_copy(
             src_ref=src, dst_ref=dst, send_sem=send, recv_sem=recv,
@@ -71,17 +88,27 @@
     for g in range(kv_heads):
         for copy in local_copies(g):
             copy.start()
+    for g in range(kv_heads):
+        for copy in loads(g):
+            copy.start()
     pl.semaphore_wait(barrier, 3)
     for g in range(kv_heads):
         for copy in local_copies(g):
             copy.wait()
-        copy_a(g).start()
+        if g == 0:
+            copy_a(g).start()
 
         @pl.when(even)
         def _():
             copy_b(g, here).start()
 
     parts[:, blocks * slots] = jnp.zeros((2, BLOCK, HD), jnp.float32)
+    for b in range(blocks):
+        for w in range((R_DEV + 1) * blocks):
+            found = jnp.int32(blocks * slots)
+            for s in range(slots):
+                found = jnp.where(lists_ref[b, s] == window_base + w, b * slots + s, found)
+            inverse[b, w] = jnp.where(window_base + w >= 0, found, blocks * slots)
     first = me * (blocks * BLOCK)
     lanes = lax.broadcasted_iota(jnp.int32, (1, BLOCK), 1)
     rows = lax.broadcasted_iota(jnp.int32, (BLOCK, BLOCK), 0)
@@ -92,9 +119,12 @@
             start = starts_ref[d]
             low = jnp.maximum(low, jnp.where(start <= pos, start, 0))
         for s in range(slots):
-            at = base_ref[b, s] + rows
+            entry = lists_ref[b, s]
+            at = jnp.where(entry >= 0, entry * BLOCK, FAR) + rows
             keep = jnp.logical_and(at <= pos, at >= low)
             bias[b, pl.ds(s * BLOCK, BLOCK), :] = jnp.where(keep, 0.0, -1e30)
+    copy_a(0).wait_send()
+    copy_a(1).start()
 
     def arrive(g):
         copy_a(g).wait_recv()
@@ -112,13 +142,17 @@
 
     def attend(g, b):
         cols = pl.ds(pl.multiple_of(g * (groups * HD), groups * HD), groups * HD)
-        picks = [index_ref[b, s] for s in range(slots)]
+        picks = []
+        for s in range(slots):
+            entry = lists_ref[b, s]
+            spot = jnp.where(entry >= 0, entry - window_base, R_DEV * blocks)
+            picks.append(jnp.clip(spot, 0, (R_DEV + 1) * blocks - 1))
         keys = jnp.concatenate([current[0, w] for w in picks], axis=0)
         values = jnp.concatenate([current[1, w] for w in picks], axis=0)
         keys_t = jnp.concatenate([turned[0, w] for w in picks], axis=1)
         values_t = jnp.concatenate([turned[1, w] for w in picks], axis=1)
-        query_all = query_ref[b, :, cols]
-        grad_all = grad_ref[b, :, cols]
+        query_all = query_buf[b, :, cols]
+        grad_all = grad_buf[b, :, cols]
         mask = jnp.concatenate([bias[b], bias[b]], axis=1)
         dkeys = dvalues = None
         for pair in range(groups // 2):
@@ -143,8 +177,8 @@
             ).astype(jnp.bfloat16)
             for at, j in enumerate(tiles):
                 spot = pl.ds(pl.multiple_of(g * (groups * HD) + j * HD, HD), HD)
-                out_ref[b, :, spot] = out_t[:, at * BLOCK:(at + 1) * BLOCK].T
-                dquery_ref[b, :, spot] = dquery_t[:, at * BLOCK:(at + 1) * BLOCK].T
+                out_buf[b, :, spot] = out_t[:, at * BLOCK:(at + 1) * BLOCK].T
+                dquery_buf[b, :, spot] = dquery_t[:, at * BLOCK:(at + 1) * BLOCK].T
             dkey = jnp.dot(dscores, query, preferred_element_type=jnp.float32)
             dvalue = jnp.dot(low, grad, preferred_element_type=jnp.float32)
             dkeys = dkey if dkeys is None else dkeys + dkey
@@ -154,6 +188,8 @@
 
     def head(g, _):
         copy_b(g, here).wait_recv()
+        for copy in loads(g):
+            copy.wait()
         for kind in range(2):
             for w in range((R_DEV + 1) * blocks):
                 tile = window[g, kind, w]
@@ -161,36 +197,50 @@
                 turned[kind, w] = tile.T
 
         def block(b, _):
-            @pl.when(jnp.logical_and(b == blocks - 1, g < kv_heads - 1))
+            @pl.when(b == blocks // 2)
             def _():
-                arrive(g + 1)
-
-            @pl.when(jnp.logical_and(jnp.logical_and(b == 1, g > 0), odd))
-            def _():
-                forward_grad(g - 1)
+                @pl.when(g < kv_heads - 2)
+                def _():
+                    copy_a(g + 1).wait_send()
+                    copy_a(g + 2).start()
+
+                @pl.when(g < kv_heads - 1)
+                def _():
+                    arrive(g + 1)
+
+                @pl.when(jnp.logical_and(g > 0, odd))
+                def _():
+                    forward_grad(g - 1)
 
             attend(g, b)
             return 0
 
         lax.fori_loop(0, blocks, block, 0)
         for kind in range(2):
-            for w in range(2 * blocks):
-                total = parts[kind, inverse_ref[0, w]]
+            for w in range(blocks, 2 * blocks):
+                total = parts[kind, inverse[0, w]]
                 for b in range(1, blocks):
-                    total = total + parts[kind, inverse_ref[b, w]]
-                into, at = (send_a, w) if w < blocks else (send_b, w - blocks)
-                into[g, kind, at] = total.astype(jnp.bfloat16)
+                    total = total + parts[kind, inverse[b, w]]
+                send_b[g, kind, w - blocks] = total.astype(jnp.bfloat16)
         grad_b(g).start()
+        for kind in range(2):
+            for w in range(blocks):
+                total = parts[kind, inverse[0, w]]
+                for b in range(1, blocks):
+                    total = total + parts[kind, inverse[b, w]]
+                send_a[g, kind, w] = total.astype(jnp.bfloat16)
 
         @pl.when(even)
         def _():
             grad_a(g).start()
 
+        for copy in stores(g):
+            copy.start()
         for kind in range(2):
             for j in range(blocks):
                 total = parts[kind, j * slots]
                 for b in range(j + 1, blocks):
-                    total = total + parts[kind, inverse_ref[b, 2 * blocks + j]]
+                    total = total + parts[kind, inverse[b, 2 * blocks + j]]
                 own[g, kind, j] = total
         return 0
 
@@ -213,9 +263,8 @@
             ref[:, :, cols] = (own[g, kind] + take_a[g, kind].astype(jnp.float32)).astype(
                 jnp.bfloat16
             )
-    for g in range(kv_heads):
-        copy_a(g).wait_send()
-
+    copy_a(kv_heads - 1).wait_send()
+    for g in range(kv_heads):
         @pl.when(even)
         def _():
             copy_b(g, here).wait_send()
@@ -226,22 +275,16 @@
 
         grad_a(g).wait_send()
         grad_b(g).wait_send()
+        for copy in stores(g):
+            copy.wait()
 
 
 def per_device(n, queries, keys, values, out_grad, doc_starts, block_lists):
-    device = lax.axis_index("ctx")
     blocks, slots = block_lists.shape
     rows = queries.shape[0]
     kv_heads = keys.shape[1] // HD
     groups = queries.shape[1] // keys.shape[1]
     window_blocks = (R_DEV + 1) * blocks
-    listed = block_lists >= 0
-    at = block_lists - (device - R_DEV) * blocks
-    index = jnp.where(listed, at, R_DEV * blocks)
-    base = jnp.where(listed, block_lists * BLOCK, FAR)
-    hit = (at[:, :, None] == jnp.arange(window_blocks)[None, None, :]) & listed[:, :, None]
-    place = jnp.arange(blocks)[:, None, None] * slots + jnp.arange(slots)[None, :, None]
-    inverse = jnp.min(jnp.where(hit, place, blocks * slots), axis=1).astype(jnp.int32)
     wide, slim = queries.shape[1], keys.shape[1]
 
     def shaped(array):
@@ -261,8 +304,8 @@
             jax.ShapeDtypeStruct((blocks, BLOCK, slim), bf16),
             jax.ShapeDtypeStruct((blocks, BLOCK, slim), bf16),
         ),
-        in_specs=[smem] * 4 + [hbm] * 2 + [vmem] * 2,
-        out_specs=[vmem] * 4,
+        in_specs=[smem] * 2 + [hbm] * 4,
+        out_specs=[hbm] * 2 + [vmem] * 2,
         scratch_shapes=[
             pltpu.VMEM((kv_heads, 2, window_blocks, BLOCK, HD), bf16),
             pltpu.VMEM((2, window_blocks, BLOCK, HD), bf16),
@@ -274,8 +317,9 @@
             pltpu.VMEM(chunk, bf16),
             pltpu.VMEM(chunk, bf16),
             pltpu.VMEM(chunk, bf16),
-            dma((kv_heads, 2)),
-        ] + [dma((kv_heads,))] * 8,
+        ] + [pltpu.VMEM((blocks, BLOCK, wide), bf16)] * 4 + [
+            pltpu.SMEM((blocks, window_blocks), jnp.int32),
+        ] + [dma((kv_heads, 2))] * 3 + [dma((kv_heads,))] * 8,
         compiler_params=pltpu.CompilerParams(
             collective_id=0, has_side_effects=True, vmem_limit_bytes=56 * 1024 * 1024
         ),
@@ -285,8 +329,7 @@
             transcendentals=rows * (wide // HD) * slots * BLOCK,
         ),
     )(
-        index.astype(jnp.int32), base.astype(jnp.int32), inverse, doc_starts,
-        shaped(keys), shaped(values), shaped(queries), shaped(out_grad),
+        block_lists, doc_starts, shaped(keys), shaped(values), shaped(queries), shaped(out_grad),
     )
     return tuple(result.reshape(rows, result.shape[2]) for result in results)
 

time: 75.9 us -> 72.5 us (0.955)
  other arithmetic: 3.21 us -> 0 us
    select_n x2 -> x0, other arithmetic: 2.53 us -> none  [the longest x1 1.26 us: per_device(): base = jnp.where(listed, block_lists * BLOCK, FAR)]
where the time goes in v3:
time: 72.5 us; the launch traced here: 72.3 us
  Pallas kernels  65.4 us (90%)
  local copies, waits for them, and re-layouts  6.27 us (9%)
    pallas_call x1, Pallas kernels, per_device(): pl.pallas_call(functools.partial(kernel, n, blocks, slots, kv_heads, grou...  65.4 us
    unnamed x10, local copies, waits for them, and re-layouts  6.27 us

profile of v3, /device:TPU:1, one launch (start us, length us, event | category | flops | bytes accessed | tf_op | source)
XLA Modules:
  0.0 72.3 jit_solution(9862615569959941387)
XLA Ops:
  0.6 65.4 %shard_map.93 = (bf16[4,128,2048]{2,1,0:T(8,128)(2,1)}, bf16[4,128,2048]{2,1,0:T(8,128)(2,1)}, bf16[4,128,512]{2,1,0:T(8,128)(2,1)}, bf16[4,128,512]{2,1,0:T(8,128)(2,1)}) custom-call(s32[4,6]{1,0:T(4,128)} %lists_ref.1, s32[8]{0:T(128)} %starts_ref.1, bf16[4,128,512]{2,1,0:T(8,128)(2,1)} %bitcast.14, bf16[4,128,512]{2,1,0:T(8,128)(2,1)} %bitcast.15, ...), custom_call_target="tpu_custom_call" | custom-call | flops 9663676416 | bytes 10485760 | tf_op jit(solution)/shard_map/pallas_call | solution.py:299
  66.0 0.0 copy-start
  66.1 3.3 %copy.14 = bf16[512,2048]{1,0:T(8,128)(2,1)} copy(bf16[512,2048]{1,0:T(8,128)(2,1)} %bitcast.9) | data formatting | bytes 4194304
  69.4 0.0 copy-done
  69.4 0.0 copy-start.2
  69.4 0.0 copy-start.1
  69.4 1.3 %copy.15 = bf16[512,2048]{1,0:T(8,128)(2,1)} copy(bf16[512,2048]{1,0:T(8,128)(2,1)S(1)} %bitcast.8) | data formatting | bytes 4194304
  70.7 0.1 copy-done.2
  70.7 0.8 %copy.16 = bf16[512,512]{1,0:T(8,128)(2,1)} copy(bf16[512,512]{1,0:T(8,128)(2,1)S(1)} %bitcast.11) | data formatting | bytes 1048576
  71.5 0.0 copy-done.1
  71.5 0.8 %copy.17 = bf16[512,512]{1,0:T(8,128)(2,1)} copy(bf16[512,512]{1,0:T(8,128)(2,1)S(1)} %bitcast.10) | data formatting | bytes 1048576
Async XLA Ops:
  66.0 3.3 %copy-start = (bf16[4,128,2048]{2,1,0:T(8,128)(2,1)S(1)}, bf16[4,128,2048]{2,1,0:T(8,128)(2,1)}, u32[]{:S(2)}) copy-start(bf16[4,128,2048]{2,1,0:T(8,128)(2,1)} %get-tuple-element.9) | copy-start | bytes 6291460
  69.4 1.4 %copy-start.2 = (bf16[4,128,512]{2,1,0:T(8,128)(2,1)S(1)}, bf16[4,128,512]{2,1,0:T(8,128)(2,1)}, u32[]{:S(2)}) copy-start(bf16[4,128,512]{2,1,0:T(8,128)(2,1)} %get-tuple-element.10) | copy-start | bytes 1572868
  69.4 2.2 %copy-start.1 = (bf16[4,128,512]{2,1,0:T(8,128)(2,1)S(1)}, bf16[4,128,512]{2,1,0:T(8,128)(2,1)}, u32[]{:S(2)}) copy-start(bf16[4,128,512]{2,1,0:T(8,128)(2,1)} %get-tuple-element.11) | copy-start | bytes 1572868

commit v4 on v3

--- a/solution.py
+++ b/solution.py
@@ -153,36 +153,36 @@
         values_t = jnp.concatenate([turned[1, w] for w in picks], axis=1)
         query_all = query_buf[b, :, cols]
         grad_all = grad_buf[b, :, cols]
-        mask = jnp.concatenate([bias[b], bias[b]], axis=1)
-        dkeys = dvalues = None
-        for pair in range(groups // 2):
-            tiles = [2 * pair, 2 * pair + 1]
-            query = jnp.concatenate([query_all[:, j * HD:(j + 1) * HD] for j in tiles], axis=0)
-            grad = jnp.concatenate([grad_all[:, j * HD:(j + 1) * HD] for j in tiles], axis=0)
-            nt = (((1,), (1,)), ((), ()))
-            scores = lax.dot_general(keys, query, nt, preferred_element_type=jnp.float32)
-            dprobs = lax.dot_general(values, grad, nt, preferred_element_type=jnp.float32)
-            scores = scores * scale2 + mask
-            top = jnp.max(scores, axis=0, keepdims=True)
-            probs = jnp.exp2(scores - top)
-            probs = probs * (1.0 / jnp.sum(probs, axis=0, keepdims=True))
-            low = probs.astype(jnp.bfloat16)
-            out_t = jnp.dot(values_t, low, preferred_element_type=jnp.float32).astype(jnp.bfloat16)
-            delta = jnp.sum(
-                out_t.astype(jnp.float32) * grad.T.astype(jnp.float32), axis=0, keepdims=True
-            )
-            dscores = (probs * (dprobs - delta)).astype(jnp.bfloat16)
-            dquery_t = (
-                jnp.dot(keys_t, dscores, preferred_element_type=jnp.float32) * scaling
-            ).astype(jnp.bfloat16)
-            for at, j in enumerate(tiles):
-                spot = pl.ds(pl.multiple_of(g * (groups * HD) + j * HD, HD), HD)
-                out_buf[b, :, spot] = out_t[:, at * BLOCK:(at + 1) * BLOCK].T
-                dquery_buf[b, :, spot] = dquery_t[:, at * BLOCK:(at + 1) * BLOCK].T
-            dkey = jnp.dot(dscores, query, preferred_element_type=jnp.float32)
-            dvalue = jnp.dot(low, grad, preferred_element_type=jnp.float32)
-            dkeys = dkey if dkeys is None else dkeys + dkey
-            dvalues = dvalue if dvalues is None else dvalues + dvalue
+        mask = jnp.concatenate([bias[b]] * groups, axis=1)
+        query = jnp.concatenate(
+            [query_all[:, j * HD:(j + 1) * HD] for j in range(groups)], axis=0
+        )
+        grad = jnp.concatenate([grad_all[:, j * HD:(j + 1) * HD] for j in range(groups)], axis=0)
+        grad_t = jnp.concatenate(
+            [grad_all[:, j * HD:(j + 1) * HD].T for j in range(groups)], axis=1
+        )
+        nt = (((1,), (1,)), ((), ()))
+        scores = lax.dot_general(keys, query, nt, preferred_element_type=jnp.float32)
+        dprobs = jnp.dot(values, grad_t, preferred_element_type=jnp.float32)
+        scores = scores * scale2 + mask
+        top = jnp.max(scores, axis=0, keepdims=True)
+        probs = jnp.exp2(scores - top)
+        probs = probs * (1.0 / jnp.sum(probs, axis=0, keepdims=True))
+        low = probs.astype(jnp.bfloat16)
+        out_t = jnp.dot(values_t, low, preferred_element_type=jnp.float32).astype(jnp.bfloat16)
+        delta = jnp.sum(
+            out_t.astype(jnp.float32) * grad_t.astype(jnp.float32), axis=0, keepdims=True
+        )
+        dscores = (probs * (dprobs - delta)).astype(jnp.bfloat16)
+        dvalues = jnp.dot(low, grad, preferred_element_type=jnp.float32)
+        dquery_t = (
+            jnp.dot(keys_t, dscores, preferred_element_type=jnp.float32) * scaling
+        ).astype(jnp.bfloat16)
+        dkeys = jnp.dot(dscores, query, preferred_element_type=jnp.float32)
+        for j in range(groups):
+            spot = pl.ds(pl.multiple_of(g * wide + j * HD, HD), HD)
+            out_buf[b, :, spot] = out_t[:, j * BLOCK:(j + 1) * BLOCK].T
+            dquery_buf[b, :, spot] = dquery_t[:, j * BLOCK:(j + 1) * BLOCK].T
         parts[0, pl.ds(b * slots, slots)] = (dkeys * scaling).reshape(slots, BLOCK, HD)
         parts[1, pl.ds(b * slots, slots)] = dvalues.reshape(slots, BLOCK, HD)
 
@@ -197,20 +197,18 @@
                 turned[kind, w] = tile.T
 
         def block(b, _):
-            @pl.when(b == blocks // 2)
+            @pl.when(jnp.logical_and(b == 1, g < kv_heads - 2))
             def _():
-                @pl.when(g < kv_heads - 2)
-                def _():
-                    copy_a(g + 1).wait_send()
-                    copy_a(g + 2).start()
-
-                @pl.when(g < kv_heads - 1)
-                def _():
-                    arrive(g + 1)
-
-                @pl.when(jnp.logical_and(g > 0, odd))
-                def _():
-                    forward_grad(g - 1)
+                copy_a(g + 1).wait_send()
+                copy_a(g + 2).start()
+
+            @pl.when(jnp.logical_and(b == 1, jnp.logical_and(g > 0, odd)))
+            def _():
+                forward_grad(g - 1)
+
+            @pl.when(jnp.logical_and(b == blocks - 1, g < kv_heads - 1))
+            def _():
+                arrive(g + 1)
 
             attend(g, b)
             return 0
@@ -277,6 +275,19 @@
         grad_b(g).wait_send()
         for copy in stores(g):
             copy.wait()
+
+
+def copy_kernel(*refs):
+    sems = refs[8]
+    copies = [
+        pltpu.make_async_copy(refs[i].at[b], refs[4 + i].at[b], sems.at[i, b])
+        for i in range(4)
+        for b in range(refs[i].shape[0])
+    ]
+    for copy in copies:
+        copy.start()
+    for copy in copies:
+        copy.wait()
 
 
 def per_device(n, queries, keys, values, out_grad, doc_starts, block_lists):
@@ -331,6 +342,14 @@
     )(
         block_lists, doc_starts, shaped(keys), shaped(values), shaped(queries), shaped(out_grad),
     )
+    results = pl.pallas_call(
+        copy_kernel,
+        out_shape=tuple(jax.ShapeDtypeStruct(result.shape, bf16) for result in results),
+        in_specs=[hbm] * 4,
+        out_specs=[hbm] * 4,
+        scratch_shapes=[dma((4, blocks))],
+        compiler_params=pltpu.CompilerParams(vmem_limit_bytes=56 * 1024 * 1024),
+    )(*results)
     return tuple(result.reshape(rows, result.shape[2]) for result in results)
 
 

time: 72.5 us -> 228 us (3.14)
  Pallas kernels: 65.4 us -> 227 us
  local copies, waits for them, and re-layouts: 6.27 us -> 0 us
    pallas_call x0 -> x1, Pallas kernels: none -> 160 us  [per_device(): pl.pallas_call(copy_kernel, out_shape=tuple((jax.ShapeDtypeStruct(result....]
    unnamed x10 -> x0, local copies, waits for them, and re-layouts: 6.27 us -> none
where the time goes in v4:
time: 228 us
  Pallas kernels  227 us (100%)
    pallas_call x1, Pallas kernels, per_device(): pl.pallas_call(copy_kernel, out_shape=tuple((jax.ShapeDtypeStruct(result....  160 us
    pallas_call x1, Pallas kernels, per_device(): pl.pallas_call(functools.partial(kernel, n, blocks, slots, kv_heads, grou...  66.9 us

profile of v4, /device:TPU:1, one launch (start us, length us, event | category | flops | bytes accessed | tf_op | source)
XLA Modules:
  0.0 227.6 jit_solution(12130441438021808900)
XLA Ops:
  0.6 66.9 %shard_map.93 = (bf16[4,128,2048]{2,1,0:T(8,128)(2,1)}, bf16[4,128,2048]{2,1,0:T(8,128)(2,1)}, bf16[4,128,512]{2,1,0:T(8,128)(2,1)}, bf16[4,128,512]{2,1,0:T(8,128)(2,1)}) custom-call(s32[4,6]{1,0:T(4,128)} %lists_ref.1, s32[8]{0:T(128)} %starts_ref.1, bf16[4,128,512]{2,1,0:T(8,128)(2,1)} %bitcast.12, bf16[4,128,512]{2,1,0:T(8,128)(2,1)} %bitcast.13, ...), custom_call_target="tpu_custom_call" | custom-call | flops 9663676416 | bytes 10485760 | tf_op jit(solution)/shard_map/pallas_call | solution.py:310
  67.5 160.1 %shard_map.94 = (bf16[4,128,2048]{2,1,0:T(8,128)(2,1)}, bf16[4,128,2048]{2,1,0:T(8,128)(2,1)}, bf16[4,128,512]{2,1,0:T(8,128)(2,1)}, bf16[4,128,512]{2,1,0:T(8,128)(2,1)}) custom-call(bf16[4,128,2048]{2,1,0:T(8,128)(2,1)} %get-tuple-element.12.refs_0_, bf16[4,128,2048]{2,1,0:T(8,128)(2,1)} %get-tuple-element.13.refs_1_, ...), custom_call_target="tpu_custom_call" | custom-call | tf_op jit(solution)/shard_map/pallas_call | solution.py:345

commit v5 on v4

--- a/solution.py
+++ b/solution.py
@@ -278,16 +278,8 @@
 
 
 def copy_kernel(*refs):
-    sems = refs[8]
-    copies = [
-        pltpu.make_async_copy(refs[i].at[b], refs[4 + i].at[b], sems.at[i, b])
-        for i in range(4)
-        for b in range(refs[i].shape[0])
-    ]
-    for copy in copies:
-        copy.start()
-    for copy in copies:
-        copy.wait()
+    for source, result in zip(refs[:4], refs[4:]):
+        result[...] = source[...]
 
 
 def per_device(n, queries, keys, values, out_grad, doc_starts, block_lists):
@@ -342,12 +334,16 @@
     )(
         block_lists, doc_starts, shaped(keys), shaped(values), shaped(queries), shaped(out_grad),
     )
+
+    def half_block(result):
+        return pl.BlockSpec((1, BLOCK // 2, result.shape[2]), lambda i: (i // 2, i % 2, 0))
+
     results = pl.pallas_call(
         copy_kernel,
         out_shape=tuple(jax.ShapeDtypeStruct(result.shape, bf16) for result in results),
-        in_specs=[hbm] * 4,
-        out_specs=[hbm] * 4,
-        scratch_shapes=[dma((4, blocks))],
+        grid=(rows // (BLOCK // 2),),
+        in_specs=[half_block(result) for result in results],
+        out_specs=[half_block(result) for result in results],
         compiler_params=pltpu.CompilerParams(vmem_limit_bytes=56 * 1024 * 1024),
     )(*results)
     return tuple(result.reshape(rows, result.shape[2]) for result in results)

time: 228 us -> 74.8 us (0.33)
  Pallas kernels: 227 us -> 73.9 us
    pallas_call x1, Pallas kernels: 160 us -> 7.01 us  [per_device(): pl.pallas_call(copy_kernel, out_shape=tuple((jax.ShapeDtypeStruct(result....]
where the time goes in v5:
time: 74.8 us; the launch traced here: 74.5 us
  Pallas kernels  73.9 us (99%)
    pallas_call x1, Pallas kernels, per_device(): pl.pallas_call(functools.partial(kernel, n, blocks, slots, kv_heads, grou...  66.9 us
    pallas_call x1, Pallas kernels, per_device(): pl.pallas_call(copy_kernel, out_shape=tuple((jax.ShapeDtypeStruct(result....  7.01 us

profile of v5, /device:TPU:1, one launch (start us, length us, event | category | flops | bytes accessed | tf_op | source)
XLA Modules:
  0.0 74.5 jit_solution(964555458868306732)
XLA Ops:
  0.6 66.9 %shard_map.93 = (bf16[4,128,2048]{2,1,0:T(8,128)(2,1)}, bf16[4,128,2048]{2,1,0:T(8,128)(2,1)}, bf16[4,128,512]{2,1,0:T(8,128)(2,1)}, bf16[4,128,512]{2,1,0:T(8,128)(2,1)}) custom-call(s32[4,6]{1,0:T(4,128)} %lists_ref.1, s32[8]{0:T(128)} %starts_ref.1, bf16[4,128,512]{2,1,0:T(8,128)(2,1)} %bitcast.12, bf16[4,128,512]{2,1,0:T(8,128)(2,1)} %bitcast.13, ...), custom_call_target="tpu_custom_call" | custom-call | flops 9663676416 | bytes 10485760 | tf_op jit(solution)/shard_map/pallas_call | solution.py:302
  67.5 7.0 %shard_map.94 = (bf16[4,128,2048]{2,1,0:T(8,128)(2,1)}, bf16[4,128,2048]{2,1,0:T(8,128)(2,1)}, bf16[4,128,512]{2,1,0:T(8,128)(2,1)}, bf16[4,128,512]{2,1,0:T(8,128)(2,1)}) custom-call(bf16[4,128,2048]{2,1,0:T(8,128)(2,1)} %get-tuple-element.12.refs_0_, bf16[4,128,2048]{2,1,0:T(8,128)(2,1)} %get-tuple-element.13.refs_1_, ...), custom_call_target="tpu_custom_call" | custom-call | tf_op jit(solution)/shard_map/pallas_call | solution.py:341
